TPU v7x, 32 devices: a whole 2x2x4 slice. The times are simulated.
32 devices in a mesh: slab: 4 (over y, x), member: 8 (over z, core).
Axes of the slice: x: 2, y: 2, z: 4, core: 2. Of those that a mesh axis runs over, the one named last changes fastest.
Arguments:
- initial: float32 [64, 512, 1024], P('member', 'slab'), may hold values from -6 to 6
- stencil_numbers: float32 [3, 512, 1024], P(None, 'slab'), may hold values from -0.25 to 0.25, as said below
- innovations: float32 [64, 131072], P(None, ('slab', 'member')), may hold values from -6 to 6
- obs_prec: float32 [131072], P(('slab', 'member')), may hold values from 0.05 to 0.5
- obs_cell: int32 [4096, 32], P(('slab', 'member')), may hold values from 0 to 127
- band_idx: int32 [4096, 9], P(('slab', 'member')), may hold values from 0 to 4095, as said below
Outputs:
- analysis: float32 [64, 512, 1024], P('member', 'slab')
Inputs may be any that keep to these rules, and one draw needn't show every extreme that they name: stencil_numbers[0] lies in 0.08 to 0.2; stencil_numbers[1] and stencil_numbers[2] lie in -0.25 to 0.25. `band_idx`: row b holds 9 distinct block indices j with |j - b| <= 8.
All inputs are finite; a program needn't handle non-finite values.
Results may differ from a plain program's by a relative error of at most 0.00011.
Values sent between devices are 32-bit elements; how exact they have to be, the bound alone decides.
No kernel may reach another device: no remote copies, remote signals or barrier semaphores. Data moves between devices by JAX's collectives and lax.ppermute only.
A program may use at most 128 MiB of HBM per device.

v0:
```python
import jax
import jax.numpy as jnp
from jax import lax
from jax.sharding import PartitionSpec as P

STEPS = 4
OB = 32
R = 8


exact = lax.Precision.HIGHEST


def with_halo(block, sides, width):
    for axis, dim in sides:
        count = lax.axis_size(axis)
        forward = [(i, i + 1) for i in range(count - 1)]
        backward = [(target, source) for source, target in forward]
        low = lax.ppermute(
            lax.slice_in_dim(block, block.shape[dim] - width, None, axis=dim), axis, forward
        )
        high = lax.ppermute(lax.slice_in_dim(block, 0, width, axis=dim), axis, backward)
        block = jnp.concatenate([low, block, high], axis=dim)
    return block


def from_behind(block, axis, distance):
    devices = range(lax.axis_size(axis))
    route = [(i - distance, i) for i in devices if i - distance in devices]
    return lax.ppermute(block, axis, route)


def advance(padded, stencil_numbers):
    centre = padded[:, 1:-1, :]
    north_cell = padded[:, 2:, :]
    south_cell = padded[:, :-2, :]
    east_cell = jnp.roll(centre, -1, axis=2)
    west_cell = jnp.roll(centre, 1, axis=2)
    spread = east_cell + west_cell + north_cell + south_cell - 4.0 * centre
    return (
        centre
        + stencil_numbers[0] * spread
        - 0.5 * stencil_numbers[1] * (east_cell - west_cell)
        - 0.5 * stencil_numbers[2] * (north_cell - south_cell)
    )


def shards(initial, stencil_numbers, innovations, obs_prec, obs_cell, band_idx):
    stacked = jnp.concatenate([initial, stencil_numbers], axis=0)
    padded = with_halo(stacked, (("slab", 1),), STEPS)
    fields = padded[: initial.shape[0]]
    coeff_ext = padded[initial.shape[0] :]
    height = coeff_ext.shape[1]
    for step_no in range(STEPS):
        fields = advance(fields, coeff_ext[:, step_no + 1 : height - step_no - 1, :])
    groups = lax.axis_size("member")
    mem_count, lat_rows, lon_cells = fields.shape
    tile_cells = lat_rows * lon_cells // groups
    outgoing = fields.reshape(mem_count, groups, tile_cells)
    gathered = lax.all_to_all(outgoing, "member", split_axis=1, concat_axis=0, tiled=True).reshape(
        mem_count * groups, tile_cells
    )
    members = gathered.shape[0]
    tile_blocks = tile_cells // 128
    partition_shape = gathered.reshape(members, tile_blocks, 128)
    ensemble_mean = jnp.mean(partition_shape, axis=0)
    anomaly = partition_shape - ensemble_mean
    lane_ids = jnp.arange(128, dtype=jnp.int32)
    picker = (lane_ids[None, :, None] == obs_cell[:, None, :]).astype(jnp.float32)
    observed = jnp.einsum("mbc,bco->mbo", anomaly, picker, precision=exact)
    weighted = innovations.reshape(members, tile_blocks, OB) * obs_prec.reshape(tile_blocks, OB)
    first_block = lax.axis_index(("slab", "member")) * tile_blocks
    extent = tile_blocks + 2 * R
    local_band = band_idx - first_block + R
    own_blocks = first_block + jnp.arange(tile_blocks, dtype=jnp.int32)
    distance = jnp.abs(band_idx - own_blocks[:, None]).astype(jnp.float32)
    tapers = 1.0 - distance / (R + 1.0)
    slot_ids = jnp.arange(extent, dtype=jnp.int32)
    selector = (slot_ids[None, None, :] == local_band[:, :, None]).astype(jnp.float32)
    mixing = jnp.einsum("xjo,mjo->jxm", observed, weighted, precision=exact)
    prev_rims = from_behind(mixing[tile_blocks - R :], ("slab", "member"), 1)
    next_rims = from_behind(mixing[:R], ("slab", "member"), -1)
    extended = jnp.concatenate([prev_rims, mixing, next_rims], axis=0)
    band_weight = jnp.einsum("bke,bk->be", selector, tapers, precision=exact)
    summed = jnp.einsum("be,exy->bxy", band_weight, extended, precision=exact)
    increment = jnp.einsum("bxm,xbc->mbc", summed, anomaly, precision=exact) / (members - 1)
    updated = (partition_shape + increment).reshape(members, 1, tile_cells)
    returned = lax.all_to_all(updated, "member", split_axis=0, concat_axis=1, tiled=True)
    return returned.reshape(mem_count, lat_rows, lon_cells)


def solution(mesh):
    in_specs = (
        P("member", "slab", None),
        P(None, "slab", None),
        P(None, ("slab", "member")),
        P(("slab", "member")),
        P(("slab", "member"), None),
        P(("slab", "member"), None),
    )
    out_specs = P("member", "slab", None)
    return jax.shard_map(shards, mesh=mesh, in_specs=in_specs, out_specs=out_specs, check_vma=False)
```

profile of v0, /device:TPU:0, one launch (start us, length us, event | category | flops | bytes accessed | tf_op | source)
XLA Modules:
  0.0 350.7 jit_solution(17105649489467674747)
XLA Ops:
  0.0 2.6 constant_dynamic-update-slice_fusion.1
  2.9 4.9 %collective-permute-start = (f32[11,4,1024]{2,1,0:T(4,128)S(1)}, f32[11,4,1024]{2,1,0:T(4,128)S(1)}, u32[]{:S(2)}, u32[]{:S(2)}) collective-permute-start(f32[11,4,1024]{2,1,0:T(4,128)S(1)} %get-tuple-element.18), channel_id=1, source_target_pairs={{0,8},{8,16},{16,24},{1,9},{9,17},{17,25},{2,10},{10,18},{18,26},{... | collective-permute-start | bytes 540680 | tf_op jit(solution)/shard_map/ppermute | solution.py:19
  11.5 5.8 %collective-permute-done.1 = f32[11,4,1024]{2,1,0:T(4,128)S(1)} collective-permute-done((f32[11,4,1024]{2,1,0:T(4,128)S(1)}, f32[11,4,1024]{2,1,0:T(4,128)S(1)}, u32[]{:S(2)}, u32[]{:S(2)}) %collective-permute-start.1) | collective-permute-done | bytes 180256 | tf_op jit(solution)/shard_map/ppermute | solution.py:22
  19.9 2.6 fusion.17
  22.7 5.9 %multiply_subtract_fusion.2 = f32[8,134,1024]{2,1,0:T(8,128)S(1)} fusion(f32[11,136,1024]{2,1,0:T(8,128)S(1)} %pad_maximum_fusion, f32[8,134,1023]{2,1,0:T(8,128)S(1)} %get-tuple-element.15, f32[8,134,1]{2,1,0:T(8,128)S(1)} %get-tuple-element.17, f32[8,134,1]{2,1,0:T(8,128)S(1)} %get-tuple-element.16, f32[8,134,1023]{2,1,0:T(8,128)S(1)} %get-tuple-element.14, ...), kind=kLoop, calls=%fused_computation.10 | loop fusion | flops 16465920 | bytes 27992064 | tf_op jit(solution)/shard_map/sub | solution.py:41
  28.6 4.3 %fusion.24 = (f32[8,132,1023]{2,1,0:T(8,128)S(1)}, f32[8,132,1023]{2,1,0:T(8,128)}) fusion(f32[8,134,1024]{2,1,0:T(8,128)S(1)} %multiply_subtract_fusion.2), kind=kLoop, calls=%fused_computation.60 | loop fusion | bytes 17284608 | tf_op jit(solution)/shard_map/jit(_roll_static)/slice | solution.py:37
  34.1 5.0 %multiply_subtract_fusion.1 = f32[8,132,1024]{2,1,0:T(8,128)S(1)} fusion(f32[8,134,1024]{2,1,0:T(8,128)S(1)} %multiply_subtract_fusion.2, f32[8,132,1023]{2,1,0:T(8,128)} %get-tuple-element.29, f32[8,132,1]{2,1,0:T(8,128)} %get-tuple-element.31, f32[8,132,1]{2,1,0:T(8,128)S(1)} %get-tuple-element.30, f32[8,132,1023]{2,1,0:T(8,128)S(1)} %get-tuple-element.28, ...), kind=kLoop, calls=%fused_computation.9 | loop fusion | flops 16220160 | bytes 27574272 | tf_op jit(solution)/shard_map/sub | solution.py:41
  39.1 2.6 fusion.22
  44.0 5.5 %multiply_subtract_fusion = f32[8,130,1024]{2,1,0:T(8,128)S(1)} fusion(f32[8,132,1024]{2,1,0:T(8,128)S(1)} %multiply_subtract_fusion.1, f32[8,130,1023]{2,1,0:T(8,128)S(1)} %get-tuple-element.25, f32[8,130,1]{2,1,0:T(8,128)} %get-tuple-element.27, f32[8,130,1]{2,1,0:T(8,128)} %get-tuple-element.26, f32[8,130,1023]{2,1,0:T(8,128)S(1)} %get-tuple-element.24, ...), kind=kLoop, calls=%fused_computation.8 | loop fusion | flops 15974400 | bytes 27156480 | tf_op jit(solution)/shard_map/sub | solution.py:41
  49.5 2.5 fusion.20
  52.2 4.6 %multiply_subtract_fusion.3 = f32[8,128,1024]{2,1,0:T(8,128)} fusion(f32[8,130,1024]{2,1,0:T(8,128)S(1)} %multiply_subtract_fusion, f32[8,128,1023]{2,1,0:T(8,128)S(1)} %get-tuple-element.21, f32[8,128,1]{2,1,0:T(8,128)S(1)} %get-tuple-element.23, f32[8,128,1]{2,1,0:T(8,128)S(1)} %get-tuple-element.22, f32[8,128,1023]{2,1,0:T(8,128)S(1)} %get-tuple-element.20, ...), kind=kLoop, calls=%fused_computation.15 | loop fusion | flops 15728640 | bytes 26738688 | tf_op jit(solution)/shard_map/sub | solution.py:41
  56.8 4.9 %reshape.30 = f32[8,8,16384]{2,1,0:T(8,128)} reshape(f32[8,128,1024]{2,1,0:T(8,128)} %multiply_subtract_fusion.3) | data formatting | bytes 8388608 | tf_op jit(solution)/shard_map/reshape | solution.py:59
  61.7 6.6 %copy.40 = f32[8,8,16384]{2,0,1:T(8,128)} copy(f32[8,8,16384]{2,1,0:T(8,128)} %reshape.30) | data formatting | bytes 8388608 | tf_op jit(solution)/shard_map/reshape | solution.py:59
  68.3 5.0 %all-to-all-start = ((f32[8,8,16384]{2,0,1:T(8,128)}), f32[8,8,16384]{2,0,1:T(8,128)}, u32[]{:S(2)}, u32[]{:S(2)}) async-start(f32[8,8,16384]{2,0,1:T(8,128)} %copy.40), calls=%async_computation | async-start | bytes 8388608 | tf_op jit(solution)/shard_map/all_to_all | solution.py:60
  74.2 93.3 %all-to-all-done = f32[8,8,16384]{2,0,1:T(8,128)} async-done(((f32[8,8,16384]{2,0,1:T(8,128)}), f32[8,8,16384]{2,0,1:T(8,128)}, u32[]{:S(2)}, u32[]{:S(2)}) %all-to-all-start) | async-done | bytes 4194336 | tf_op jit(solution)/shard_map/all_to_all | solution.py:60
  167.5 4.9 %copy.57 = f32[8,8,128,128]{3,2,1,0:T(8,128)} copy(f32[8,8,128,128]{3,1,2,0:T(8,128)} %bitcast.28) | data formatting | bytes 8388608
  172.4 2.5 reduce_sum.9
  174.9 2.5 broadcast_subtract_fusion
  177.4 7.2 %fusion = f32[128,32,64]{2,1,0:T(8,128)S(1)} fusion(f32[64,128,128]{2,1,0:T(8,128)S(1)} %broadcast_subtract_fusion, s32[128,32]{1,0:T(8,128)S(1)} %copy.41), kind=kOutput, calls=%fused_computation.16 | convolution fusion | flops 403177472 | bytes 5259264 | tf_op jit(solution)/shard_map/mbc,bco->mbo/dot_general | solution.py:70
  184.6 7.4 %fusion.6 = f32[128,64,64]{2,1,0:T(8,128)S(1)} fusion(f32[128,32,64]{2,1,0:T(8,128)S(1)} %fusion, f32[64,128,32]{0,2,1:T(8,128)S(1)} %bitcast.61, f32[128,32]{1,0:T(8,128)S(1)} %mul.246), kind=kOutput, calls=%fused_computation.20 | convolution fusion | flops 201588736 | bytes 4210688 | tf_op jit(solution)/shard_map/xjo,mjo->jxm/dot_general | solution.py:80
  192.1 1.6 collective-permute-start.2
  195.1 2.0 collective-permute-done.3
  197.1 2.6 pad_maximum_fusion.1
  199.7 6.1 %copy.44 = f32[144,64,64]{0,2,1:T(8,128)} copy(f32[144,64,64]{2,1,0:T(8,128)} %pad_maximum_fusion.1) | data formatting | bytes 4718592 | tf_op jit(solution)/shard_map/concatenate | solution.py:83
  205.8 5.2 %fusion.27 = f32[128,4096]{0,1:S(1)} fusion(f32[128,144]{0,1:T(8,128)S(1)} %select_reduce_fusion, f32[144,4096]{0,1:T(8,128)} %bitcast.57), kind=kOutput, calls=%fused_computation.63 | convolution fusion | flops 905969664 | bytes 4530176
  211.0 4.7 %copy.46 = f32[128,64,64]{1,2,0:T(8,128)} copy(f32[128,64,64]{0,2,1:T(8,128)S(1)} %bitcast.60) | data formatting | bytes 4194304 | tf_op jit(solution)/shard_map/be,exy->bxy/dot_general | solution.py:85
  215.8 13.8 %bitcast_add_fusion = f32[64,128,128]{2,0,1:T(8,128)S(1)} fusion(f32[64,128,128]{2,1,0:T(8,128)} %bitcast.56, f32[128,64,64]{1,2,0:T(8,128)} %copy.46, f32[64,128,128]{2,1,0:T(8,128)} %copy-done), kind=kOutput, calls=%fused_computation.14 | convolution fusion | flops 807403520 | bytes 14680064 | tf_op jit(solution)/shard_map/bxm,xbc->mbc/dot_general | solution.py:86
  229.5 2.4 copy.48
  231.9 106.9 %all_to_all.30 = f32[64,1,16384]{2,1,0:T(1,128)S(1)} all-to-all(f32[64,1,16384]{2,1,0:T(1,128)S(1)} %bitcast.58), channel_id=1, replica_groups=mesh['slab'=4,'member'=8] {'member'}, dimensions={0} | all-to-all | bytes 8388608 | tf_op jit(solution)/shard_map/all_to_all | solution.py:88
  338.8 2.4 copy.66
  341.2 4.4 %copy.50 = f32[8,8,1,16384]{3,1,0,2:T(8,128)} copy(f32[8,8,1,16384]{3,0,1,2:T(8,128)S(1)} %bitcast.59) | data formatting | bytes 8388608 | tf_op jit(solution)/shard_map/all_to_all | solution.py:88
  345.6 4.9 %reshape.33 = f32[8,128,1024]{2,1,0:T(8,128)} reshape(f32[8,8,1,16384]{3,1,0,2:T(8,128)} %copy.50) | data formatting | bytes 8388608 | tf_op jit(solution)/shard_map/reshape | solution.py:89
  (42 shorter events, 12.7 us)
Async XLA Ops:
  0.0 2.7 copy-start.1
  2.9 8.6 %collective-permute-start = (f32[11,4,1024]{2,1,0:T(4,128)S(1)}, f32[11,4,1024]{2,1,0:T(4,128)S(1)}, u32[]{:S(2)}, u32[]{:S(2)}) collective-permute-start(f32[11,4,1024]{2,1,0:T(4,128)S(1)} %get-tuple-element.18), channel_id=1, source_target_pairs={{0,8},{8,16},{16,24},{1,9},{9,17},{17,25},{2,10},{10,18},{18,26},{... | collective-permute-start | bytes 540680 | tf_op jit(solution)/shard_map/ppermute | solution.py:19
  7.7 9.6 %collective-permute-start.1 = (f32[11,4,1024]{2,1,0:T(4,128)S(1)}, f32[11,4,1024]{2,1,0:T(4,128)S(1)}, u32[]{:S(2)}, u32[]{:S(2)}) collective-permute-start(f32[11,4,1024]{2,1,0:T(4,128)S(1)} %get-tuple-element.19), channel_id=1, source_target_pairs={{8,0},{16,8},{24,16},{9,1},{17,9},{25,17},{10,2},{18,10},{26,18},{... | collective-permute-start | bytes 540680 | tf_op jit(solution)/shard_map/ppermute | solution.py:22
  49.4 2.7 copy-start.2
  49.4 2.7 copy-start.3
  49.5 2.7 copy-start.4
  68.3 5.0 %copy-start.7 = (s32[128,32]{0,1:T(8,128)S(1)}, s32[128,32]{0,1:T(8,128)}, u32[]{:S(2)}) copy-start(s32[128,32]{0,1:T(8,128)} %param.10) | copy-start | bytes 49156
  68.3 5.1 %copy-start.5 = (f32[64,4096]{1,0:T(8,128)S(1)}, f32[64,4096]{1,0:T(8,128)}, u32[]{:S(2)}) copy-start(f32[64,4096]{1,0:T(8,128)} %param.8) | copy-start | bytes 3145732
  68.3 5.7 %copy-start.8 = (f32[4096]{0:T(1024)S(1)}, f32[4096]{0:T(1024)}, u32[]{:S(2)}) copy-start(f32[4096]{0:T(1024)} %param.9) | copy-start | bytes 49156
  68.3 5.8 %copy-start.6 = (s32[128,9]{0,1:T(8,128)S(1)}, s32[128,9]{0,1:T(8,128)}, u32[]{:S(2)}) copy-start(s32[128,9]{0,1:T(8,128)} %param.11) | copy-start | bytes 13828
  68.3 99.1 %all-to-all-start = ((f32[8,8,16384]{2,0,1:T(8,128)}), f32[8,8,16384]{2,0,1:T(8,128)}, u32[]{:S(2)}, u32[]{:S(2)}) async-start(f32[8,8,16384]{2,0,1:T(8,128)} %copy.40), calls=%async_computation | async-start | bytes 8388608 | tf_op jit(solution)/shard_map/all_to_all | solution.py:60
  177.4 14.6 %copy-start = (f32[64,128,128]{2,1,0:T(8,128)}, f32[64,128,128]{2,1,0:T(8,128)S(1)}, u32[]{:S(2)}) copy-start(f32[64,128,128]{2,1,0:T(8,128)S(1)} %broadcast_subtract_fusion) | copy-start | bytes 12582916
  192.1 3.0 collective-permute-start.2
  193.7 3.4 collective-permute-start.3
where the time goes:
time: 355 us; the launch traced here: 351 us
  blocking collectives  107 us (30%)
  waiting for transfers between devices  102 us (29%)
  local copies, waits for them, and re-layouts  59.8 us (17%)
  other arithmetic  33.6 us (9%)
  matrix products  33.5 us (9%)
  starting transfers between devices  14 us (4%)
    all_to_all x1, blocking collectives, shards(): lax.all_to_all(updated, 'member', split_axis=0, concat_axis=1, tiled=True)  107 us
    all_to_all x1, waiting for transfers between devices, shards(): lax.all_to_all(outgoing, 'member', split_axis=1, concat_axis=0, tiled=True)  93.3 us
    sub x4, other arithmetic, advance(): centre + stencil_numbers[0] * spread  20.9 us
    slice x8, local copies, waits for them, and re-layouts, advance(): east_cell = jnp.roll(centre, -1, axis=2)  14.7 us
    dot_general x1, matrix products, shards(): jnp.einsum('bxm,xbc->mbc', summed, anomaly, precision=exact) / (members - 1)  13.8 us
    reshape x2, local copies, waits for them, and re-layouts, shards(): outgoing = fields.reshape(mem_count, groups, tile_cells)  11.6 us
    unnamed x23, local copies, waits for them, and re-layouts  10.7 us
    dot_general x1, matrix products, shards(): mixing = jnp.einsum('xjo,mjo->jxm', observed, weighted, precision=exact)  7.4 us
  transfers between devices with their start and end apart: 5, of which 4 were waited for; matrix products, arithmetic and copies ran while one was open for 1% of the time, Pallas kernels for 0%

commit v1 on v0

v1 whole, which is shorter than its diff:
```python
import functools

import jax
import jax.numpy as jnp
from jax import lax
from jax.experimental import pallas as pl
from jax.experimental.pallas import tpu as pltpu
from jax.sharding import PartitionSpec as P

STEPS = 4
OB = 32
R = 8
LANES = 128
VMEM = pl.BlockSpec(memory_space=pltpu.VMEM)
SMEM = pl.BlockSpec(memory_space=pltpu.SMEM)
f32 = jnp.float32
bf16 = jnp.bfloat16


def params(mib):
    return pltpu.CompilerParams(vmem_limit_bytes=mib << 20)


def cost(flops, nbytes):
    return pl.CostEstimate(flops=int(flops), bytes_accessed=int(nbytes), transcendentals=0)


def ceil_div(a, b):
    return -(-a // b)


def partners(count, r):
    if count & (count - 1) == 0:
        return [(i, i ^ r) for i in range(count)]
    return [(i, (i + r) % count) for i in range(count)]


def partner_tables(count, me):
    r = jnp.arange(count, dtype=jnp.int32)
    if count & (count - 1) == 0:
        return me ^ r, me ^ r
    return (me + r) % count, (me - r) % count


def exchange(pieces, axis):
    count = lax.axis_size(axis)
    order = sorted(range(1, count), key=lambda r: -r)
    got = {r: lax.ppermute(pieces[r], axis, partners(count, r)) for r in order}
    return [pieces[0]] + [got[r] for r in range(1, count)]


def exchange_back(pieces, axis):
    count = lax.axis_size(axis)
    order = sorted(range(1, count), key=lambda r: -r)
    got = {
        r: lax.ppermute(pieces[r], axis, [(d, s) for s, d in partners(count, r)]) for r in order
    }
    return [pieces[0]] + [got[r] for r in range(1, count)]


def shift_blocks(block, axis, distance):
    devices = range(lax.axis_size(axis))
    route = [(i - distance, i) for i in devices if i - distance in devices]
    return lax.ppermute(block, axis, route)


def coefficients(numbers):
    k, u, v = numbers
    return (1.0 - 4.0 * k, k - 0.5 * u, k + 0.5 * u, k - 0.5 * v, k + 0.5 * v)


def step_rows(src, dst, coef, first, last, offset):
    def one_row(r, _):
        members, lon = src.shape[1:]
        here = src[r]
        east = pltpu.roll(here, lon - 1, 1)
        west = pltpu.roll(here, 1, 1)
        row = [
            jnp.broadcast_to(coef[i, pl.ds(r + offset, 1), :], (members, lon)) for i in range(5)
        ]
        dst[r] = (
            row[0] * here
            + row[1] * east
            + row[2] * west
            + row[3] * src[r + 1]
            + row[4] * src[r - 1]
        )
        return 0

    lax.fori_loop(first, last, one_row, 0, unroll=2)


def interior_kernel(plan, count, dest, q, numbers, *rest):
    early, rest_out = rest[:count], rest[count]
    buf_a, buf_b, coef = rest[count + 1 :]
    members, rows, _ = q.shape
    tile = rows // count
    for i, c in enumerate(coefficients([numbers[i] for i in range(3)])):
        coef[i] = c

    def turn(g, _):
        r = pl.multiple_of(g * 8, 8)
        buf_a[pl.ds(r, 8)] = jnp.swapaxes(q[:, pl.ds(r, 8), :], 0, 1)
        return 0

    lax.fori_loop(0, rows // 8, turn, 0)
    src, dst = buf_a, buf_b
    for s in range(STEPS):
        step_rows(src, dst, coef, s + 1, rows - s - 1, 0)
        src, dst = dst, src
    for r in range(count):
        base = dest[r] * tile
        for slot, row in enumerate(plan.early):
            early[r][slot] = src[base + row]

    def keep(t, _):
        for slot, row in enumerate(plan.late):
            rest_out[t, slot] = src[t * tile + row]
        return 0

    lax.fori_loop(0, count, keep, 0)


def border_kernel(plan, count, dest, low, high, q_low, q_high, coef_low, coef_high, kept, *rest):
    late = rest[:count]
    buf_a, buf_b, coef, final = rest[count:]
    members = q_low.shape[0]
    wide = 3 * STEPS
    final[...] = kept[...]
    for side, (halo, own, own_coef) in enumerate(
        ((low, q_low, coef_low), (high, q_high, coef_high))
    ):
        strips = (
            [(halo, 0, STEPS), (own, 0, 2 * STEPS)]
            if side == 0
            else [(own, 0, 2 * STEPS), (halo, 0, STEPS)]
        )
        at = 0
        for ref, first, n in strips:
            for r in range(n):
                buf_a[at + r] = ref[:members, first + r, :]
            at += n
        halo_numbers = [halo[members + i] for i in range(3)]
        own_numbers = [own_coef[i] for i in range(3)]
        for i, (h, o) in enumerate(zip(coefficients(halo_numbers), coefficients(own_numbers))):
            parts = [h, o] if side == 0 else [o, h]
            at = 0
            for part in parts:
                coef[i, at : at + part.shape[0], :] = part
                at += part.shape[0]
        src, dst = buf_a, buf_b
        for s in range(STEPS):
            step_rows(src, dst, coef, s + 1, wide - s - 1, 0)
            src, dst = dst, src
        for r in range(STEPS):
            tile, row = plan.where(r if side == 0 else plan.rows - STEPS + r)
            final[tile, plan.late.index(row)] = src[STEPS + r]
    for r in range(count):
        late[r][...] = final[dest[r]]


def split(x):
    high = x.astype(bf16)
    return high, (x - high.astype(f32)).astype(bf16)


def mm(a, b, dims=((1,), (0,))):
    return lax.dot_general(a, b, (dims, ((), ())), preferred_element_type=f32)


def analysis_kernel(plan, count, fresh, old_mix, old_fields, out_rows, keep_fields, *refs):
    refs = list(refs)
    take = lambda n: [refs.pop(0) for _ in range(n)]
    source, rows_of, out_of = take(3)
    pieces = take(count) if fresh else []
    inn, prec, cells = take(3) if fresh else (None, None, None)
    weights = take(1)[0] if out_rows else None
    old_mix_refs = take(len(old_mix))
    old_field_refs = take(len(old_fields))
    mix_out = take(1)[0] if fresh else None
    kept_out = take(1)[0] if keep_fields else None
    outs = take(count) if out_rows else []
    mix, fields = take(2)
    tile = plan.tile
    members, lon = fields.shape[1:]
    share = members // count
    group = LANES // OB
    pack = plan.pack
    per_row = lon // LANES
    pairs = per_row // pack
    for slots, ref in zip(old_mix, old_mix_refs):
        for row, slot in slots:
            mix[row + 1] = ref[slot]
    for slots, ref in zip(old_fields, old_field_refs):
        for row, slot in slots:
            fields[row] = ref[slot]
    if fresh:
        for r in range(count):
            first = pl.multiple_of(source[r] * share, share)
            for slot, row in enumerate(fresh):
                fields[row, pl.ds(first, share), :] = pieces[r][slot]

        def observe(slot, _):
            row = rows_of[slot]
            for q in range(per_row // group):
                anomalies = []
                for t in range(group):
                    lanes = slice((q * group + t) * LANES, (q * group + t + 1) * LANES)
                    block = fields[row, :, lanes]
                    anomalies.append(block - jnp.mean(block, axis=0, keepdims=True))
                high, low = split(jnp.concatenate(anomalies, axis=0))
                at = row * (per_row // group) + q
                cell_row = cells[pl.ds(at, 1), :]
                chosen = (
                    lax.broadcasted_iota(jnp.int32, (LANES, LANES), 0)
                    == jnp.broadcast_to(cell_row, (LANES, LANES))
                )
                pick = jnp.where(chosen, 1.0, 0.0).astype(bf16)
                seen = mm(high, pick) + mm(low, pick)
                shape = seen.shape
                same = (
                    lax.broadcasted_iota(jnp.int32, shape, 0) // members
                    == lax.broadcasted_iota(jnp.int32, shape, 1) // OB
                )
                seen_high, seen_low = split(jnp.where(same, seen, 0.0))
                lanes = pl.ds(pl.multiple_of(at * LANES, LANES), LANES)
                weighted = inn[:, lanes] * prec[:, lanes]
                w_high, w_low = split(weighted)
                both = mm(
                    jnp.concatenate([w_high, w_low], axis=0), seen_high, ((1,), (1,))
                )
                total = both[:members] + both[members:] + mm(w_high, seen_low, ((1,), (1,)))
                wide = pack * members
                for k in range(group // pack):
                    mix[row + 1, q * (group // pack) + k] = total[:, k * wide : (k + 1) * wide]
            return 0

        lax.fori_loop(0, len(fresh), observe, 0)
        for slot, row in enumerate(fresh):
            mix_out[slot] = mix[row + 1]
    for slot, row in enumerate(keep_fields):
        kept_out[slot] = fields[row]
    if out_rows:
        reach = ceil_div(R, pack)
        width = 2 * reach + 1

        def update(slot, _):
            row = out_of[slot]
            for pair in range(pairs):
                sums = [jnp.zeros((members, pack * members), f32) for _ in range(pack)]
                for d in range(width):
                    place = pair + d - reach
                    step = place // pairs
                    part = mix[row + 1 + step, place - step * pairs]
                    for t in range(pack):
                        block = row * per_row + pair * pack + t
                        w = weights[block, pl.ds(d, 1), :]
                        sums[t] += part * jnp.broadcast_to(w, part.shape)
                for t in range(pack):
                    first = (pair * pack + t) * LANES
                    cells_here = fields[row, :, first : first + LANES]
                    anomaly = cells_here - jnp.mean(cells_here, axis=0, keepdims=True)
                    a_high, a_low = split(anomaly)
                    a_high = jnp.concatenate([a_high] * pack, axis=0)
                    a_low = jnp.concatenate([a_low] * pack, axis=0)
                    s_high, s_low = split(sums[t])
                    both = mm(jnp.concatenate([s_high, s_low], axis=0), a_high)
                    done = cells_here + both[:members] + both[members:] + mm(s_high, a_low)
                    fields[row, :, first : first + LANES] = done
            return 0

        lax.fori_loop(0, len(out_rows), update, 0)
        for r in range(count):
            first = pl.multiple_of(source[r] * share, share)
            for slot, row in enumerate(out_rows):
                outs[r][slot] = fields[row, pl.ds(first, share), :]


def assemble_kernel(plan, count, parts, source, *refs):
    pieces, (out, buf) = refs[:-2], refs[-2:]
    at = 0
    for rows in parts:
        for r in range(count):
            base = source[r] * plan.tile
            for slot, row in enumerate(rows):
                buf[base + row] = pieces[at + r][slot]
        at += count

    def turn(g, _):
        r = pl.multiple_of(g * 8, 8)
        out[:, pl.ds(r, 8), :] = jnp.swapaxes(buf[pl.ds(r, 8)], 0, 1)
        return 0

    lax.fori_loop(0, plan.rows // 8, turn, 0)


class Plan:
    def __init__(self, rows, count, members):
        self.rows = rows
        self.count = count
        self.tile = rows // count
        self.members = members
        self.pack = max(1, LANES // members)
        tile = self.tile
        self.early = [r for r in range(tile) if STEPS <= r < tile - STEPS]
        self.late = [r for r in range(tile) if r not in self.early]

    def where(self, row):
        return row // self.tile, row % self.tile


def shards(initial, stencil_numbers, innovations, obs_prec, obs_cell, band_idx):
    share, rows, lon = initial.shape
    count = lax.axis_size("member")
    members = share * count
    plan = Plan(rows, count, members)
    tile, pack = plan.tile, plan.pack
    per_row = lon // LANES
    pairs = per_row // pack
    me = lax.axis_index("member")
    dest, source = partner_tables(count, me)
    sds = lambda *shape: jax.ShapeDtypeStruct(shape, f32)
    ints = lambda values: jnp.array(list(values) or [0], jnp.int32)

    stacked_low = jnp.concatenate([initial[:, :STEPS], stencil_numbers[:, :STEPS]], axis=0)
    stacked_high = jnp.concatenate([initial[:, -STEPS:], stencil_numbers[:, -STEPS:]], axis=0)
    low = shift_blocks(stacked_high, "slab", 1)
    high = shift_blocks(stacked_low, "slab", -1)

    early_rows, late_rows = len(plan.early), len(plan.late)
    outs = pl.pallas_call(
        functools.partial(interior_kernel, plan, count),
        out_shape=[sds(max(early_rows, 1), share, lon)] * count
        + [sds(count, late_rows, share, lon)],
        in_specs=[SMEM, VMEM, VMEM],
        out_specs=[VMEM] * (count + 1),
        scratch_shapes=[
            pltpu.VMEM((rows, share, lon), f32),
            pltpu.VMEM((rows, share, lon), f32),
            pltpu.VMEM((5, rows, lon), f32),
        ],
        compiler_params=params(40),
        cost_estimate=cost(11 * STEPS * initial.size, 8 * initial.size),
        name="interior",
    )(dest, initial, stencil_numbers)
    early, kept = outs[:count], outs[count]
    if plan.early:
        early = exchange(early, "member")

    late = pl.pallas_call(
        functools.partial(border_kernel, plan, count),
        out_shape=[sds(late_rows, share, lon)] * count,
        in_specs=[SMEM] + [VMEM] * 7,
        out_specs=[VMEM] * count,
        scratch_shapes=[
            pltpu.VMEM((3 * STEPS, share, lon), f32),
            pltpu.VMEM((3 * STEPS, share, lon), f32),
            pltpu.VMEM((5, 3 * STEPS, lon), f32),
            pltpu.VMEM((count, late_rows, share, lon), f32),
        ],
        compiler_params=params(40),
        cost_estimate=cost(11 * STEPS * initial.size // 4, 4 * initial.size),
        name="border",
    )(
        dest,
        low,
        high,
        initial[:, : 2 * STEPS],
        initial[:, -2 * STEPS :],
        stencil_numbers[:, : 2 * STEPS],
        stencil_numbers[:, -2 * STEPS :],
        kept,
    )
    late = exchange(late, "member")

    blocks = tile * per_row
    first_block = lax.axis_index(("slab", "member")) * blocks
    own = first_block + jnp.arange(blocks, dtype=jnp.int32)
    reach = ceil_div(R, pack)
    width = 2 * reach + 1
    start = own // pack * pack - reach * pack
    reached = start[:, None] + jnp.arange(width * pack, dtype=jnp.int32)
    in_band = jnp.any(reached[:, :, None] == band_idx[:, None, :], axis=2)
    distance = jnp.abs(reached - own[:, None]).astype(f32)
    tapers = jnp.where(in_band, 1.0 - distance / (R + 1.0), 0.0) / (members - 1)
    weights = jnp.repeat(tapers, members, axis=1).reshape(blocks, width, pack * members)
    prec = obs_prec.reshape(1, -1)
    cells = obs_cell.reshape(-1, LANES)

    def analyse(fresh, pieces, old_mix, old_fields, out_rows, keep_fields, name):
        args = [source, ints(fresh), ints(out_rows)]
        specs = [SMEM] * 3
        shapes = []
        if fresh:
            args += [*pieces, innovations, prec, cells]
            shapes += [sds(len(fresh), pairs, members, pack * members)]
        if out_rows:
            args += [weights]
        args += [m[1] for m in old_mix] + [f[1] for f in old_fields]
        if keep_fields:
            shapes += [sds(len(keep_fields), members, lon)]
        if out_rows:
            shapes += [sds(len(out_rows), share, lon)] * count
        specs += [VMEM] * (len(args) - 3)
        got = list(
            pl.pallas_call(
                functools.partial(
                    analysis_kernel,
                    plan,
                    count,
                    fresh,
                    [m[0] for m in old_mix],
                    [f[0] for f in old_fields],
                    out_rows,
                    keep_fields,
                ),
                out_shape=shapes,
                in_specs=specs,
                out_specs=[VMEM] * len(shapes),
                scratch_shapes=[
                    pltpu.VMEM((tile + 2, pairs, members, pack * members), f32),
                    pltpu.VMEM((tile, members, lon), f32),
                ],
                compiler_params=params(56),
                cost_estimate=cost(
                    (len(fresh) + len(out_rows)) * 6 * members * members * lon,
                    4 * members * lon * (len(fresh) + 2 * len(out_rows)),
                ),
                name=name,
            )(*args)
        )
        mixing = got.pop(0) if fresh else None
        kept_fields = got.pop(0) if keep_fields else None
        return mixing, kept_fields, got

    slots = lambda rows: [(row, slot) for slot, row in enumerate(rows)]
    parts, returned = [], []
    rims = sorted({0, tile - 1})
    inner = [r for r in plan.early if r - 1 in plan.early and r + 1 in plan.early]
    old_mix, old_fields = [], []
    if plan.early:
        edge = [r for r in plan.early if r not in inner]
        mixing, fields, back = analyse(plan.early, early, [], [], inner, edge, "analyse_early")
        old_mix = [(slots(plan.early), mixing)]
        old_fields = [(slots(edge), fields)] if edge else []
        if inner:
            parts.append(inner)
            returned += exchange_back(back, "member")
    middle = [r for r in range(tile) if r not in inner and r not in rims]
    mixing, fields, back = analyse(
        plan.late, late, old_mix, old_fields, middle, rims, "analyse_late"
    )
    axes = ("slab", "member")
    from_prev = shift_blocks(mixing[plan.late.index(tile - 1)][None], axes, 1)
    from_next = shift_blocks(mixing[plan.late.index(0)][None], axes, -1)
    if middle:
        parts.append(middle)
        returned += exchange_back(back, "member")
    near = sorted({row for r in rims for row in (r - 1, r, r + 1) if 0 <= row < tile})
    near_late = [r for r in near if r in plan.late]
    held = [([(-1, 0)], from_prev), ([(tile, 0)], from_next)]
    held.append(([(row, plan.late.index(row)) for row in near_late], mixing))
    _, _, back = analyse([], [], held, [(slots(rims), fields)], rims, [], "analyse_rims")
    parts.append(rims)
    returned += exchange_back(back, "member")

    return pl.pallas_call(
        functools.partial(assemble_kernel, plan, count, parts),
        out_shape=sds(share, rows, lon),
        in_specs=[SMEM] + [VMEM] * len(returned),
        out_specs=VMEM,
        scratch_shapes=[pltpu.VMEM((rows, share, lon), f32)],
        compiler_params=params(40),
        cost_estimate=cost(0, 8 * initial.size),
        name="assemble",
    )(source, *returned)


def solution(mesh):
    in_specs = (
        P("member", "slab", None),
        P(None, "slab", None),
        P(None, ("slab", "member")),
        P(("slab", "member")),
        P(("slab", "member"), None),
        P(("slab", "member"), None),
    )
    out_specs = P("member", "slab", None)
    return jax.shard_map(shards, mesh=mesh, in_specs=in_specs, out_specs=out_specs, check_vma=False)
```

time: 355 us -> 253 us (0.71)
  the two profiles are of different devices: /device:TPU:0 before, /device:TPU:11 now
where the time goes in v1:
time: 253 us
  waiting for transfers between devices  120 us (47%)
  Pallas kernels  63.1 us (25%)
  starting transfers between devices  57.5 us (23%)
  local copies, waits for them, and re-layouts  11.2 us (4%)
    ppermute x21, waiting for transfers between devices, exchange_back(): lax.ppermute(pieces[r], axis, [(d, s) for s, d in partners(count, r)])  48 us
    ppermute x14, waiting for transfers between devices, exchange(): got = {r: lax.ppermute(pieces[r], axis, partners(count, r)) for r in order}  47.7 us
    pallas_call x1, Pallas kernels, shards(): pl.pallas_call(functools.partial(interior_kernel, plan, count), out_shape...  29 us
    ppermute x21, starting transfers between devices, exchange_back(): lax.ppermute(pieces[r], axis, [(d, s) for s, d in partners(count, r)])  28.1 us
    pallas_call x3, Pallas kernels, analyse(): pl.pallas_call(functools.partial(analysis_kernel, plan, count, fresh, [m[...  25.6 us
    ppermute x4, waiting for transfers between devices, shift_blocks(): return lax.ppermute(block, axis, route)  24.6 us
    ppermute x14, starting transfers between devices, exchange(): got = {r: lax.ppermute(pieces[r], axis, partners(count, r)) for r in order}  18.1 us
    ppermute x4, starting transfers between devices, shift_blocks(): return lax.ppermute(block, axis, route)  11.3 us
  transfers between devices with their start and end apart: 39, of which 18 were waited for; matrix products, arithmetic and copies ran while one was open for 2% of the time, Pallas kernels for 12%

profile of v1, /device:TPU:11, one launch (start us, length us, event | category | flops | bytes accessed | tf_op | source)
XLA Modules:
  0.0 253.0 jit_solution(6765192126173014061)
XLA Ops:
  3.6 29.0 %interior.1 = (f32[8,8,1024]{2,1,0:T(8,128)S(1)}, f32[8,8,1024]{2,1,0:T(8,128)}, f32[8,8,1024]{2,1,0:T(8,128)}, f32[8,8,1024]{2,1,0:T(8,128)}, f32[8,8,1024]{2,1...) custom-call(s32[8]{0:T(128)S(1)} %iota_xor_fusion.dest.refs_0_.sourc, ...), custom_call_target="tpu_custom_call" | custom-call | flops 46137344 | bytes 8388608 | tf_op jit(solution)/shard_map/interior/pallas_call | solution.py:331
  35.1 2.3 collective-permute-start.3
  37.5 3.1 %collective-permute-start.14 = (f32[11,4,1024]{2,1,0:T(4,128)S(1)}, f32[11,4,1024]{2,1,0:T(4,128)S(1)}, u32[]{:S(2)}, u32[]{:S(2)}) collective-permute-start(f32[11,4,1024]{2,1,0:T(4,128)S(1)} %pad_maximum_fusion), channel_id=1, source_target_pairs={{0,8},{8,16},{16,24},{1,9},{9,17},{17,25},{2,10},{10,18},{18,26},{... | collective-permute-start | bytes 540680 | tf_op jit(solution)/shard_map/ppermute | solution.py:64
  40.8 4.4 %collective-permute-done.14.low = f32[11,4,1024]{2,1,0:T(4,128)S(1)} collective-permute-done((f32[11,4,1024]{2,1,0:T(4,128)S(1)}, f32[11,4,1024]{2,1,0:T(4,128)S(1)}, u32[]{:S(2)}, u32[]{:S(2)}) %collective-permute-start.14) | collective-permute-done | bytes 180256 | tf_op jit(solution)/shard_map/ppermute | solution.py:64
  48.1 4.9 %collective-permute-done.15.high = f32[11,4,1024]{2,1,0:T(4,128)S(1)} collective-permute-done((f32[11,4,1024]{2,1,0:T(4,128)S(1)}, f32[11,4,1024]{2,1,0:T(4,128)S(1)}, u32[]{:S(2)}, u32[]{:S(2)}) %collective-permute-start.15) | collective-permute-done | bytes 180256 | tf_op jit(solution)/shard_map/ppermute | solution.py:64
  54.9 4.8 %border.1 = (f32[8,8,1024]{2,1,0:T(8,128)S(1)}, f32[8,8,1024]{2,1,0:T(8,128)S(1)}, f32[8,8,1024]{2,1,0:T(8,128)S(1)}, f32[8,8,1024]{2,1,0:T(8,128)}, f32[8,8,102...) custom-call(s32[8]{0:T(128)S(1)} %iota_xor_fusion.dest.refs_0_.source, ...), custom_call_target="tpu_custom_call" | custom-call | flops 11534336 | bytes 4194304 | tf_op jit(solution)/shard_map/border/pallas_call | solution.py:350
  64.4 13.7 %collective-permute-done.4.refs_8_ = f32[8,8,1024]{2,1,0:T(8,128)S(1)} collective-permute-done((f32[8,8,1024]{2,1,0:T(8,128)}, f32[8,8,1024]{2,1,0:T(8,128)S(1)}, u32[]{:S(2)}, u32[]{:S(2)}) %collective-permute-start.4) | collective-permute-done | bytes 262176 | tf_op jit(solution)/shard_map/ppermute | solution.py:48
  78.1 3.4 %collective-permute-start.18 = (f32[8,8,1024]{2,1,0:T(8,128)}, f32[8,8,1024]{2,1,0:T(8,128)S(1)}, u32[]{:S(2)}, u32[]{:S(2)}) collective-permute-start(f32[8,8,1024]{2,1,0:T(8,128)} %get-tuple-element.70), channel_id=1, source_target_pairs={{0,3},{1,2},{2,1},{3,0},{4,7},{5,6},{6,5},{7,4},{8,11},{9,10},{10,... | collective-permute-start | bytes 786440 | tf_op jit(solution)/shard_map/ppermute | solution.py:48
  81.5 3.9 %collective-permute-done.5.refs_9_ = f32[8,8,1024]{2,1,0:T(8,128)S(1)} collective-permute-done((f32[8,8,1024]{2,1,0:T(8,128)}, f32[8,8,1024]{2,1,0:T(8,128)S(1)}, u32[]{:S(2)}, u32[]{:S(2)}) %collective-permute-start.5) | collective-permute-done | bytes 262176 | tf_op jit(solution)/shard_map/ppermute | solution.py:48
  85.3 9.6 %collective-permute-done.6.refs_10_ = f32[8,8,1024]{2,1,0:T(8,128)S(1)} collective-permute-done((f32[8,8,1024]{2,1,0:T(8,128)}, f32[8,8,1024]{2,1,0:T(8,128)S(1)}, u32[]{:S(2)}, u32[]{:S(2)}) %collective-permute-start.6) | collective-permute-done | bytes 262176 | tf_op jit(solution)/shard_map/ppermute | solution.py:48
  101.2 10.3 %analyse_early.1 = (f32[8,4,64,128]{3,2,1,0:T(8,128)}, f32[2,64,1024]{2,1,0:T(8,128)}, f32[6,8,1024]{2,1,0:T(8,128)}, f32[6,8,1024]{2,1,0:T(8,128)}, f32[6,8,102...) custom-call(s32[8]{0:T(128)} %copy-done.7, ...), custom_call_target="tpu_custom_call" | custom-call | flops 352321536 | bytes 5242880 | tf_op jit(solution)/shard_map/analyse_early/pallas_call | solution.py:406
  111.7 5.7 %collective-permute-done.19.refs_7_ = f32[8,8,1024]{2,1,0:T(8,128)S(1)} collective-permute-done((f32[8,8,1024]{2,1,0:T(8,128)}, f32[8,8,1024]{2,1,0:T(8,128)S(1)}, u32[]{:S(2)}, u32[]{:S(2)}) %collective-permute-start.19) | collective-permute-done | bytes 262176 | tf_op jit(solution)/shard_map/ppermute | solution.py:48
  117.4 2.8 %collective-permute-start.8 = (f32[6,8,1024]{2,1,0:T(8,128)}, f32[6,8,1024]{2,1,0:T(8,128)S(1)}, u32[]{:S(2)}, u32[]{:S(2)}) collective-permute-start(f32[6,8,1024]{2,1,0:T(8,128)} %get-tuple-element.60), channel_id=1, source_target_pairs={{2,0},{3,1},{0,2},{1,3},{6,4},{7,5},{4,6},{5,7},{10,8},{11,9},{8,1... | collective-permute-start | bytes 589832 | tf_op jit(solution)/shard_map/ppermute | solution.py:56
  120.2 2.9 %collective-permute-done.20.refs_8_ = f32[8,8,1024]{2,1,0:T(8,128)S(1)} collective-permute-done((f32[8,8,1024]{2,1,0:T(8,128)}, f32[8,8,1024]{2,1,0:T(8,128)S(1)}, u32[]{:S(2)}, u32[]{:S(2)}) %collective-permute-start.20) | collective-permute-done | bytes 262176 | tf_op jit(solution)/shard_map/ppermute | solution.py:48
  123.1 3.4 %collective-permute-start.9 = (f32[6,8,1024]{2,1,0:T(8,128)}, f32[6,8,1024]{2,1,0:T(8,128)S(1)}, u32[]{:S(2)}, u32[]{:S(2)}) collective-permute-start(f32[6,8,1024]{2,1,0:T(8,128)} %get-tuple-element.61), channel_id=1, source_target_pairs={{3,0},{2,1},{1,2},{0,3},{7,4},{6,5},{5,6},{4,7},{11,8},{10,9},{9,1... | collective-permute-start | bytes 589832 | tf_op jit(solution)/shard_map/ppermute | solution.py:56
  126.4 3.9 %collective-permute-done.21.refs_9_ = f32[8,8,1024]{2,1,0:T(8,128)S(1)} collective-permute-done((f32[8,8,1024]{2,1,0:T(8,128)S(1)}, f32[8,8,1024]{2,1,0:T(8,128)S(1)}, u32[]{:S(2)}, u32[]{:S(2)}) %collective-permute-start.21) | collective-permute-done | bytes 262176 | tf_op jit(solution)/shard_map/ppermute | solution.py:48
  130.3 8.1 %collective-permute-done.22.refs_10_ = f32[8,8,1024]{2,1,0:T(8,128)S(1)} collective-permute-done((f32[8,8,1024]{2,1,0:T(8,128)S(1)}, f32[8,8,1024]{2,1,0:T(8,128)S(1)}, u32[]{:S(2)}, u32[]{:S(2)}) %collective-permute-start.22) | collective-permute-done | bytes 262176 | tf_op jit(solution)/shard_map/ppermute | solution.py:48
  139.2 11.8 %analyse_late.1 = (f32[8,4,64,128]{3,2,1,0:T(8,128)}, f32[2,64,1024]{2,1,0:T(8,128)}, f32[8,8,1024]{2,1,0:T(8,128)}, f32[8,8,1024]{2,1,0:T(8,128)}, f32[8,8,1024...) custom-call(s32[8]{0:T(128)} %copy-done.7, ...), custom_call_target="tpu_custom_call" | custom-call | flops 402653184 | bytes 6291456 | tf_op jit(solution)/shard_map/analyse_late/pallas_call | solution.py:406
  151.9 4.4 %collective-permute-start.30 = (f32[1,4,64,128]{3,2,1,0:T(8,128)S(1)}, f32[1,4,64,128]{3,2,1,0:T(8,128)S(1)}, u32[]{:S(2)}, u32[]{:S(2)}) collective-permute-start(f32[1,4,64,128]{3,2,1,0:T(8,128)S(1)} %get-tuple-element.104), channel_id=1, source_target_pairs={{0,1},{1,2},{2,3},{3,4},{4,5},{5,6},{6,7},{7,8},{8,9},{9,10},{10,1... | collective-permute-start | bytes 393224 | tf_op jit(solution)/shard_map/ppermute | solution.py:64
  159.6 2.2 collective-permute-start.13
  161.8 15.3 %collective-permute-done.31.refs_5_ = f32[1,4,64,128]{3,2,1,0:T(8,128)S(1)} collective-permute-done((f32[1,4,64,128]{3,2,1,0:T(8,128)S(1)}, f32[1,4,64,128]{3,2,1,0:T(8,128)S(1)}, u32[]{:S(2)}, u32[]{:S(2)}) %collective-permute-start.31) | collective-permute-done | bytes 131104 | tf_op jit(solution)/shard_map/ppermute | solution.py:64
  177.7 3.5 %analyse_rims.1 = (f32[2,8,1024]{2,1,0:T(8,128)}, f32[2,8,1024]{2,1,0:T(8,128)}, f32[2,8,1024]{2,1,0:T(8,128)}, f32[2,8,1024]{2,1,0:T(8,128)}, f32[2,8,1024]{2,1...) custom-call(s32[8]{0:T(128)} %copy-done.7, s32[1]{0:T(128)} %constant.60.clone.refs_1_, ...), custom_call_target="tpu_custom_call" | custom-call | flops 50331648 | bytes 1048576 | tf_op jit(solution)/shard_map/analyse_rims/pallas_call | solution.py:406
  182.7 3.5 %collective-permute-done.13.refs_7_ = f32[6,8,1024]{2,1,0:T(8,128)S(1)} collective-permute-done((f32[6,8,1024]{2,1,0:T(8,128)S(1)}, f32[6,8,1024]{2,1,0:T(8,128)S(1)}, u32[]{:S(2)}, u32[]{:S(2)}) %collective-permute-start.13) | collective-permute-done | bytes 196640 | tf_op jit(solution)/shard_map/ppermute | solution.py:56
  192.8 3.1 %collective-permute-start.38 = (f32[2,8,1024]{2,1,0:T(8,128)}, f32[2,8,1024]{2,1,0:T(8,128)S(1)}, u32[]{:S(2)}, u32[]{:S(2)}) collective-permute-start(f32[2,8,1024]{2,1,0:T(8,128)} %get-tuple-element.94), channel_id=1, source_target_pairs={{7,0},{6,1},{5,2},{4,3},{3,4},{2,5},{1,6},{0,7},{15,8},{14,9},{13,... | collective-permute-start | bytes 196616 | tf_op jit(solution)/shard_map/ppermute | solution.py:56
  196.0 2.3 collective-permute-start.25
  200.1 4.9 %collective-permute-start.27 = (f32[8,8,1024]{2,1,0:T(8,128)}, f32[8,8,1024]{2,1,0:T(8,128)S(1)}, u32[]{:S(2)}, u32[]{:S(2)}) collective-permute-start(f32[8,8,1024]{2,1,0:T(8,128)} %get-tuple-element.82), channel_id=1, source_target_pairs={{5,0},{4,1},{7,2},{6,3},{1,4},{0,5},{3,6},{2,7},{13,8},{12,9},{15,... | collective-permute-start | bytes 786440 | tf_op jit(solution)/shard_map/ppermute | solution.py:56
  205.6 4.1 %collective-permute-done.25.refs_11_ = f32[8,8,1024]{2,1,0:T(8,128)S(1)} collective-permute-done((f32[8,8,1024]{2,1,0:T(8,128)}, f32[8,8,1024]{2,1,0:T(8,128)S(1)}, u32[]{:S(2)}, u32[]{:S(2)}) %collective-permute-start.25) | collective-permute-done | bytes 262176 | tf_op jit(solution)/shard_map/ppermute | solution.py:56
  209.8 19.5 %collective-permute-done.26.refs_12_ = f32[8,8,1024]{2,1,0:T(8,128)S(1)} collective-permute-done((f32[8,8,1024]{2,1,0:T(8,128)}, f32[8,8,1024]{2,1,0:T(8,128)S(1)}, u32[]{:S(2)}, u32[]{:S(2)}) %collective-permute-start.26) | collective-permute-done | bytes 262176 | tf_op jit(solution)/shard_map/ppermute | solution.py:56
  229.3 5.6 %collective-permute-done.27.refs_13_ = f32[8,8,1024]{2,1,0:T(8,128)S(1)} collective-permute-done((f32[8,8,1024]{2,1,0:T(8,128)}, f32[8,8,1024]{2,1,0:T(8,128)S(1)}, u32[]{:S(2)}, u32[]{:S(2)}) %collective-permute-start.27) | collective-permute-done | bytes 262176 | tf_op jit(solution)/shard_map/ppermute | solution.py:56
  234.9 7.0 %collective-permute-done.28.refs_14_ = f32[8,8,1024]{2,1,0:T(8,128)S(1)} collective-permute-done((f32[8,8,1024]{2,1,0:T(8,128)}, f32[8,8,1024]{2,1,0:T(8,128)S(1)}, u32[]{:S(2)}, u32[]{:S(2)}) %collective-permute-start.28) | collective-permute-done | bytes 262176 | tf_op jit(solution)/shard_map/ppermute | solution.py:56
  242.0 5.6 %collective-permute-done.29.refs_15_ = f32[8,8,1024]{2,1,0:T(8,128)S(1)} collective-permute-done((f32[8,8,1024]{2,1,0:T(8,128)}, f32[8,8,1024]{2,1,0:T(8,128)S(1)}, u32[]{:S(2)}, u32[]{:S(2)}) %collective-permute-start.29) | collective-permute-done | bytes 262176 | tf_op jit(solution)/shard_map/ppermute | solution.py:56
  249.4 3.7 %assemble.1 = f32[8,128,1024]{2,1,0:T(8,128)} custom-call(s32[8]{0:T(128)S(1)} %copy-done.8, f32[6,8,1024]{2,1,0:T(8,128)S(1)} %copy-done.5, f32[6,8,1024]{2,1,0:T(8,128)S(1)} %collective-permute-done.7.refs_1_, f32[6,8,1024]{2,1,0:T(8,128)S(1)} %collective-permute-done.8.refs_2_, f32[6,8,1024]{2,1,0:T(8,128)S(1)} %collective-permute-done.9.refs_3_, ...), custom_call_target="tpu_custom_call" | custom-call | bytes 8388608 | tf_op jit(solution)/shard_map/assemble/pallas_call | solution.py:467
  (125 shorter events, 39.9 us)
Async XLA Ops:
  32.6 27.8 %collective-permute-start = (f32[8,8,1024]{2,1,0:T(8,128)}, f32[8,8,1024]{2,1,0:T(8,128)}, u32[]{:S(2)}, u32[]{:S(2)}) collective-permute-start(f32[8,8,1024]{2,1,0:T(8,128)} %get-tuple-element.51), channel_id=1, source_target_pairs={{0,1},{1,0},{2,3},{3,2},{4,5},{5,4},{6,7},{7,6},{8,9},{9,8},{10,11... | collective-permute-start | bytes 786440 | tf_op jit(solution)/shard_map/ppermute | solution.py:48
  33.4 28.3 %collective-permute-start.1 = (f32[8,8,1024]{2,1,0:T(8,128)}, f32[8,8,1024]{2,1,0:T(8,128)}, u32[]{:S(2)}, u32[]{:S(2)}) collective-permute-start(f32[8,8,1024]{2,1,0:T(8,128)} %get-tuple-element.52), channel_id=1, source_target_pairs={{0,2},{1,3},{2,0},{3,1},{4,6},{5,7},{6,4},{7,5},{8,10},{9,11},{10,... | collective-permute-start | bytes 786440 | tf_op jit(solution)/shard_map/ppermute | solution.py:48
  33.5 28.5 %collective-permute-start.2 = (f32[8,8,1024]{2,1,0:T(8,128)}, f32[8,8,1024]{2,1,0:T(8,128)}, u32[]{:S(2)}, u32[]{:S(2)}) collective-permute-start(f32[8,8,1024]{2,1,0:T(8,128)} %get-tuple-element.53), channel_id=1, source_target_pairs={{0,3},{1,2},{2,1},{3,0},{4,7},{5,6},{6,5},{7,4},{8,11},{9,10},{10,... | collective-permute-start | bytes 786440 | tf_op jit(solution)/shard_map/ppermute | solution.py:48
  35.1 27.2 %collective-permute-start.3 = (f32[8,8,1024]{2,1,0:T(8,128)}, f32[8,8,1024]{2,1,0:T(8,128)}, u32[]{:S(2)}, u32[]{:S(2)}) collective-permute-start(f32[8,8,1024]{2,1,0:T(8,128)} %get-tuple-element.54), channel_id=1, source_target_pairs={{0,4},{1,5},{2,6},{3,7},{4,0},{5,1},{6,2},{7,3},{8,12},{9,13},{10,... | collective-permute-start | bytes 786440 | tf_op jit(solution)/shard_map/ppermute | solution.py:48
  45.2 7.8 %collective-permute-start.15 = (f32[11,4,1024]{2,1,0:T(4,128)S(1)}, f32[11,4,1024]{2,1,0:T(4,128)S(1)}, u32[]{:S(2)}, u32[]{:S(2)}) collective-permute-start(f32[11,4,1024]{2,1,0:T(4,128)S(1)} %pad_maximum_fusion.1), channel_id=1, source_target_pairs={{8,0},{16,8},{24,16},{9,1},{17,9},{25,17},{10,2},{18,10},{26,18},{... | collective-permute-start | bytes 540680 | tf_op jit(solution)/shard_map/ppermute | solution.py:64
  52.9 25.1 %collective-permute-start.4 = (f32[8,8,1024]{2,1,0:T(8,128)}, f32[8,8,1024]{2,1,0:T(8,128)S(1)}, u32[]{:S(2)}, u32[]{:S(2)}) collective-permute-start(f32[8,8,1024]{2,1,0:T(8,128)} %get-tuple-element.55), channel_id=1, source_target_pairs={{0,5},{1,4},{2,7},{3,6},{4,1},{5,0},{6,3},{7,2},{8,13},{9,12},{10,... | collective-permute-start | bytes 786440 | tf_op jit(solution)/shard_map/ppermute | solution.py:48
  60.4 24.9 %collective-permute-start.5 = (f32[8,8,1024]{2,1,0:T(8,128)}, f32[8,8,1024]{2,1,0:T(8,128)S(1)}, u32[]{:S(2)}, u32[]{:S(2)}) collective-permute-start(f32[8,8,1024]{2,1,0:T(8,128)} %copy-done.10), channel_id=1, source_target_pairs={{0,6},{1,7},{2,4},{3,5},{4,2},{5,3},{6,0},{7,1},{8,14},{9,15},{10,... | collective-permute-start | bytes 786440 | tf_op jit(solution)/shard_map/ppermute | solution.py:48
  61.7 33.3 %collective-permute-start.6 = (f32[8,8,1024]{2,1,0:T(8,128)}, f32[8,8,1024]{2,1,0:T(8,128)S(1)}, u32[]{:S(2)}, u32[]{:S(2)}) collective-permute-start(f32[8,8,1024]{2,1,0:T(8,128)} %copy-done.9), channel_id=1, source_target_pairs={{0,7},{1,6},{2,5},{3,4},{4,3},{5,2},{6,1},{7,0},{8,15},{9,14},{10,... | collective-permute-start | bytes 786440 | tf_op jit(solution)/shard_map/ppermute | solution.py:48
  62.1 32.9 %collective-permute-start.16 = (f32[8,8,1024]{2,1,0:T(8,128)S(1)}, f32[8,8,1024]{2,1,0:T(8,128)S(1)}, u32[]{:S(2)}, u32[]{:S(2)}) collective-permute-start(f32[8,8,1024]{2,1,0:T(8,128)S(1)} %get-tuple-element.68), channel_id=1, source_target_pairs={{0,1},{1,0},{2,3},{3,2},{4,5},{5,4},{6,7},{7,6},{8,9},{9,8},{10,11... | collective-permute-start | bytes 786440 | tf_op jit(solution)/shard_map/ppermute | solution.py:48
  62.3 34.9 %collective-permute-start.17 = (f32[8,8,1024]{2,1,0:T(8,128)S(1)}, f32[8,8,1024]{2,1,0:T(8,128)S(1)}, u32[]{:S(2)}, u32[]{:S(2)}) collective-permute-start(f32[8,8,1024]{2,1,0:T(8,128)S(1)} %get-tuple-element.69), channel_id=1, source_target_pairs={{0,2},{1,3},{2,0},{3,1},{4,6},{5,7},{6,4},{7,5},{8,10},{9,11},{10,... | collective-permute-start | bytes 786440 | tf_op jit(solution)/shard_map/ppermute | solution.py:48
  78.1 33.5 %collective-permute-start.18 = (f32[8,8,1024]{2,1,0:T(8,128)}, f32[8,8,1024]{2,1,0:T(8,128)S(1)}, u32[]{:S(2)}, u32[]{:S(2)}) collective-permute-start(f32[8,8,1024]{2,1,0:T(8,128)} %get-tuple-element.70), channel_id=1, source_target_pairs={{0,3},{1,2},{2,1},{3,0},{4,7},{5,6},{6,5},{7,4},{8,11},{9,10},{10,... | collective-permute-start | bytes 786440 | tf_op jit(solution)/shard_map/ppermute | solution.py:48
  85.3 32.1 %collective-permute-start.19 = (f32[8,8,1024]{2,1,0:T(8,128)}, f32[8,8,1024]{2,1,0:T(8,128)S(1)}, u32[]{:S(2)}, u32[]{:S(2)}) collective-permute-start(f32[8,8,1024]{2,1,0:T(8,128)} %get-tuple-element.71), channel_id=1, source_target_pairs={{0,4},{1,5},{2,6},{3,7},{4,0},{5,1},{6,2},{7,3},{8,12},{9,13},{10,... | collective-permute-start | bytes 786440 | tf_op jit(solution)/shard_map/ppermute | solution.py:48
  94.9 28.1 %collective-permute-start.20 = (f32[8,8,1024]{2,1,0:T(8,128)}, f32[8,8,1024]{2,1,0:T(8,128)S(1)}, u32[]{:S(2)}, u32[]{:S(2)}) collective-permute-start(f32[8,8,1024]{2,1,0:T(8,128)} %get-tuple-element.72), channel_id=1, source_target_pairs={{0,5},{1,4},{2,7},{3,6},{4,1},{5,0},{6,3},{7,2},{8,13},{9,12},{10,... | collective-permute-start | bytes 786440 | tf_op jit(solution)/shard_map/ppermute | solution.py:48
  95.0 35.4 %collective-permute-start.21 = (f32[8,8,1024]{2,1,0:T(8,128)S(1)}, f32[8,8,1024]{2,1,0:T(8,128)S(1)}, u32[]{:S(2)}, u32[]{:S(2)}) collective-permute-start(f32[8,8,1024]{2,1,0:T(8,128)S(1)} %get-tuple-element.73), channel_id=1, source_target_pairs={{0,6},{1,7},{2,4},{3,5},{4,2},{5,3},{6,0},{7,1},{8,14},{9,15},{10,... | collective-permute-start | bytes 786440 | tf_op jit(solution)/shard_map/ppermute | solution.py:48
  97.1 41.3 %collective-permute-start.22 = (f32[8,8,1024]{2,1,0:T(8,128)S(1)}, f32[8,8,1024]{2,1,0:T(8,128)S(1)}, u32[]{:S(2)}, u32[]{:S(2)}) collective-permute-start(f32[8,8,1024]{2,1,0:T(8,128)S(1)} %get-tuple-element.74), channel_id=1, source_target_pairs={{0,7},{1,6},{2,5},{3,4},{4,3},{5,2},{6,1},{7,0},{8,15},{9,14},{10,... | collective-permute-start | bytes 786440 | tf_op jit(solution)/shard_map/ppermute | solution.py:48
  111.6 44.7 %collective-permute-start.7 = (f32[6,8,1024]{2,1,0:T(8,128)}, f32[6,8,1024]{2,1,0:T(8,128)S(1)}, u32[]{:S(2)}, u32[]{:S(2)}) collective-permute-start(f32[6,8,1024]{2,1,0:T(8,128)} %get-tuple-element.59), channel_id=1, source_target_pairs={{1,0},{0,1},{3,2},{2,3},{5,4},{4,5},{7,6},{6,7},{9,8},{8,9},{11,10... | collective-permute-start | bytes 589832 | tf_op jit(solution)/shard_map/ppermute | solution.py:56
  117.4 40.9 %collective-permute-start.8 = (f32[6,8,1024]{2,1,0:T(8,128)}, f32[6,8,1024]{2,1,0:T(8,128)S(1)}, u32[]{:S(2)}, u32[]{:S(2)}) collective-permute-start(f32[6,8,1024]{2,1,0:T(8,128)} %get-tuple-element.60), channel_id=1, source_target_pairs={{2,0},{3,1},{0,2},{1,3},{6,4},{7,5},{4,6},{5,7},{10,8},{11,9},{8,1... | collective-permute-start | bytes 589832 | tf_op jit(solution)/shard_map/ppermute | solution.py:56
  123.1 36.5 %collective-permute-start.9 = (f32[6,8,1024]{2,1,0:T(8,128)}, f32[6,8,1024]{2,1,0:T(8,128)S(1)}, u32[]{:S(2)}, u32[]{:S(2)}) collective-permute-start(f32[6,8,1024]{2,1,0:T(8,128)} %get-tuple-element.61), channel_id=1, source_target_pairs={{3,0},{2,1},{1,2},{0,3},{7,4},{6,5},{5,6},{4,7},{11,8},{10,9},{9,1... | collective-permute-start | bytes 589832 | tf_op jit(solution)/shard_map/ppermute | solution.py:56
  130.3 29.2 %collective-permute-start.10 = (f32[6,8,1024]{2,1,0:T(8,128)}, f32[6,8,1024]{2,1,0:T(8,128)S(1)}, u32[]{:S(2)}, u32[]{:S(2)}) collective-permute-start(f32[6,8,1024]{2,1,0:T(8,128)} %get-tuple-element.62), channel_id=1, source_target_pairs={{4,0},{5,1},{6,2},{7,3},{0,4},{1,5},{2,6},{3,7},{12,8},{13,9},{14,... | collective-permute-start | bytes 589832 | tf_op jit(solution)/shard_map/ppermute | solution.py:56
  151.9 9.8 %collective-permute-start.30 = (f32[1,4,64,128]{3,2,1,0:T(8,128)S(1)}, f32[1,4,64,128]{3,2,1,0:T(8,128)S(1)}, u32[]{:S(2)}, u32[]{:S(2)}) collective-permute-start(f32[1,4,64,128]{3,2,1,0:T(8,128)S(1)} %get-tuple-element.104), channel_id=1, source_target_pairs={{0,1},{1,2},{2,3},{3,4},{4,5},{5,6},{6,7},{7,8},{8,9},{9,10},{10,1... | collective-permute-start | bytes 393224 | tf_op jit(solution)/shard_map/ppermute | solution.py:64
  156.3 20.7 %collective-permute-start.31 = (f32[1,4,64,128]{3,2,1,0:T(8,128)S(1)}, f32[1,4,64,128]{3,2,1,0:T(8,128)S(1)}, u32[]{:S(2)}, u32[]{:S(2)}) collective-permute-start(f32[1,4,64,128]{3,2,1,0:T(8,128)S(1)} %get-tuple-element.103), channel_id=1, source_target_pairs={{1,0},{2,1},{3,2},{4,3},{5,4},{6,5},{7,6},{8,7},{9,8},{10,9},{11,1... | collective-permute-start | bytes 393224 | tf_op jit(solution)/shard_map/ppermute | solution.py:64
  158.3 22.9 %collective-permute-start.11 = (f32[6,8,1024]{2,1,0:T(8,128)S(1)}, f32[6,8,1024]{2,1,0:T(8,128)S(1)}, u32[]{:S(2)}, u32[]{:S(2)}) collective-permute-start(f32[6,8,1024]{2,1,0:T(8,128)S(1)} %copy-done.27), channel_id=1, source_target_pairs={{5,0},{4,1},{7,2},{6,3},{1,4},{0,5},{3,6},{2,7},{13,8},{12,9},{15,... | collective-permute-start | bytes 589832 | tf_op jit(solution)/shard_map/ppermute | solution.py:56
  159.5 21.7 %collective-permute-start.12 = (f32[6,8,1024]{2,1,0:T(8,128)S(1)}, f32[6,8,1024]{2,1,0:T(8,128)S(1)}, u32[]{:S(2)}, u32[]{:S(2)}) collective-permute-start(f32[6,8,1024]{2,1,0:T(8,128)S(1)} %copy-done.26), channel_id=1, source_target_pairs={{6,0},{7,1},{4,2},{5,3},{2,4},{3,5},{0,6},{1,7},{14,8},{15,9},{12,... | collective-permute-start | bytes 589832 | tf_op jit(solution)/shard_map/ppermute | solution.py:56
  159.6 26.6 %collective-permute-start.13 = (f32[6,8,1024]{2,1,0:T(8,128)S(1)}, f32[6,8,1024]{2,1,0:T(8,128)S(1)}, u32[]{:S(2)}, u32[]{:S(2)}) collective-permute-start(f32[6,8,1024]{2,1,0:T(8,128)S(1)} %copy-done.25), channel_id=1, source_target_pairs={{7,0},{6,1},{5,2},{4,3},{3,4},{2,5},{1,6},{0,7},{15,8},{14,9},{13,... | collective-permute-start | bytes 589832 | tf_op jit(solution)/shard_map/ppermute | solution.py:56
  161.8 43.3 %collective-permute-start.23 = (f32[8,8,1024]{2,1,0:T(8,128)}, f32[8,8,1024]{2,1,0:T(8,128)S(1)}, u32[]{:S(2)}, u32[]{:S(2)}) collective-permute-start(f32[8,8,1024]{2,1,0:T(8,128)} %get-tuple-element.78), channel_id=1, source_target_pairs={{1,0},{0,1},{3,2},{2,3},{5,4},{4,5},{7,6},{6,7},{9,8},{8,9},{11,10... | collective-permute-start | bytes 786440 | tf_op jit(solution)/shard_map/ppermute | solution.py:56
  177.0 28.6 %collective-permute-start.24 = (f32[8,8,1024]{2,1,0:T(8,128)}, f32[8,8,1024]{2,1,0:T(8,128)S(1)}, u32[]{:S(2)}, u32[]{:S(2)}) collective-permute-start(f32[8,8,1024]{2,1,0:T(8,128)} %get-tuple-element.79), channel_id=1, source_target_pairs={{2,0},{3,1},{0,2},{1,3},{6,4},{7,5},{4,6},{5,7},{10,8},{11,9},{8,1... | collective-permute-start | bytes 786440 | tf_op jit(solution)/shard_map/ppermute | solution.py:56
  190.6 7.7 %collective-permute-start.37 = (f32[2,8,1024]{2,1,0:T(8,128)}, f32[2,8,1024]{2,1,0:T(8,128)S(1)}, u32[]{:S(2)}, u32[]{:S(2)}) collective-permute-start(f32[2,8,1024]{2,1,0:T(8,128)} %get-tuple-element.93), channel_id=1, source_target_pairs={{6,0},{7,1},{4,2},{5,3},{2,4},{3,5},{0,6},{1,7},{14,8},{15,9},{12,... | collective-permute-start | bytes 196616 | tf_op jit(solution)/shard_map/ppermute | solution.py:56
  196.0 13.8 %collective-permute-start.25 = (f32[8,8,1024]{2,1,0:T(8,128)}, f32[8,8,1024]{2,1,0:T(8,128)S(1)}, u32[]{:S(2)}, u32[]{:S(2)}) collective-permute-start(f32[8,8,1024]{2,1,0:T(8,128)} %get-tuple-element.80), channel_id=1, source_target_pairs={{3,0},{2,1},{1,2},{0,3},{7,4},{6,5},{5,6},{4,7},{11,8},{10,9},{9,1... | collective-permute-start | bytes 786440 | tf_op jit(solution)/shard_map/ppermute | solution.py:56
  198.3 31.0 %collective-permute-start.26 = (f32[8,8,1024]{2,1,0:T(8,128)}, f32[8,8,1024]{2,1,0:T(8,128)S(1)}, u32[]{:S(2)}, u32[]{:S(2)}) collective-permute-start(f32[8,8,1024]{2,1,0:T(8,128)} %get-tuple-element.81), channel_id=1, source_target_pairs={{4,0},{5,1},{6,2},{7,3},{0,4},{1,5},{2,6},{3,7},{12,8},{13,9},{14,... | collective-permute-start | bytes 786440 | tf_op jit(solution)/shard_map/ppermute | solution.py:56
  200.1 34.9 %collective-permute-start.27 = (f32[8,8,1024]{2,1,0:T(8,128)}, f32[8,8,1024]{2,1,0:T(8,128)S(1)}, u32[]{:S(2)}, u32[]{:S(2)}) collective-permute-start(f32[8,8,1024]{2,1,0:T(8,128)} %get-tuple-element.82), channel_id=1, source_target_pairs={{5,0},{4,1},{7,2},{6,3},{1,4},{0,5},{3,6},{2,7},{13,8},{12,9},{15,... | collective-permute-start | bytes 786440 | tf_op jit(solution)/shard_map/ppermute | solution.py:56
  205.0 36.9 %collective-permute-start.28 = (f32[8,8,1024]{2,1,0:T(8,128)}, f32[8,8,1024]{2,1,0:T(8,128)S(1)}, u32[]{:S(2)}, u32[]{:S(2)}) collective-permute-start(f32[8,8,1024]{2,1,0:T(8,128)} %get-tuple-element.83), channel_id=1, source_target_pairs={{6,0},{7,1},{4,2},{5,3},{2,4},{3,5},{0,6},{1,7},{14,8},{15,9},{12,... | collective-permute-start | bytes 786440 | tf_op jit(solution)/shard_map/ppermute | solution.py:56
  205.6 41.9 %collective-permute-start.29 = (f32[8,8,1024]{2,1,0:T(8,128)}, f32[8,8,1024]{2,1,0:T(8,128)S(1)}, u32[]{:S(2)}, u32[]{:S(2)}) collective-permute-start(f32[8,8,1024]{2,1,0:T(8,128)} %get-tuple-element.84), channel_id=1, source_target_pairs={{7,0},{6,1},{5,2},{4,3},{3,4},{2,5},{1,6},{0,7},{15,8},{14,9},{13,... | collective-permute-start | bytes 786440 | tf_op jit(solution)/shard_map/ppermute | solution.py:56
  (35 other events, 836.1 us)

commit v2 on v1

v2 whole, which is shorter than its diff:
```python
import functools

import jax
import jax.numpy as jnp
from jax import lax
from jax.experimental import pallas as pl
from jax.experimental.pallas import tpu as pltpu
from jax.sharding import PartitionSpec as P

STEPS = 4
OB = 32
R = 8
LANES = 128
BATCH = 16
SECTIONS = 2
FLIGHT = 5
SECTION_MIB = 58
BORDER_MIB = 32
ANALYSIS_MIB = 56
VMEM = pl.BlockSpec(memory_space=pltpu.VMEM)
SMEM = pl.BlockSpec(memory_space=pltpu.SMEM)
HBM = pl.BlockSpec(memory_space=pltpu.HBM)
f32 = jnp.float32
bf16 = jnp.bfloat16
SHORT = ("mix_rims", "mix_late", "analyse_late")


def hint(us=0):
    return pl.CostEstimate(flops=0, bytes_accessed=int(us * 3.69e6), transcendentals=0)


def params(mib):
    return pltpu.CompilerParams(vmem_limit_bytes=mib << 20)


def ceil_div(a, b):
    return -(-a // b)


def after(value, *earlier):
    return lax.optimization_barrier((value, *earlier))[0]


class Chain:
    def __init__(self, flight):
        self.flight = flight
        self.ended = []

    def permute(self, piece, axis, route):
        if len(self.ended) >= self.flight:
            piece = after(piece, self.ended[-self.flight])
        self.ended.append(lax.ppermute(piece, axis, route))
        return self.ended[-1]

    def swap(self, piece, r):
        return self.permute(piece, "member", [(i, i ^ r) for i in range(lax.axis_size("member"))])

    def shift(self, block, axis, distance):
        devices = range(lax.axis_size(axis))
        route = [(i - distance, i) for i in devices if i - distance in devices]
        return self.permute(block, axis, route)


def coefficients(numbers):
    k, u, v = numbers
    return (1.0 - 4.0 * k, k - 0.5 * u, k + 0.5 * u, k - 0.5 * v, k + 0.5 * v)


def step_rows(src, dst, coef, first, last, offset):
    members, lon = src.shape[1:]

    def one_row(r):
        here = src[r]
        east = pltpu.roll(here, lon - 1, 1)
        west = pltpu.roll(here, 1, 1)
        row = [
            jnp.broadcast_to(coef[i, pl.ds(r + offset, 1), :], (members, lon)) for i in range(5)
        ]
        dst[r] = (
            row[0] * here
            + row[1] * east
            + row[2] * west
            + row[3] * src[r + 1]
            + row[4] * src[r - 1]
        )

    def some_rows(g, _):
        for i in range(BATCH):
            one_row(first + g * BATCH + i)
        return 0

    batches = (last - first) // BATCH
    lax.fori_loop(0, batches, some_rows, 0)
    for r in range(first + batches * BATCH, last):
        one_row(r)


def section_kernel(plan, section, place, q, numbers, *refs):
    refs = list(refs)
    size = plan.size
    early = [refs.pop(0) for _ in range(size)] if plan.early else []
    kept = refs.pop(0)
    halos = [refs.pop(0) for _ in range(2)] if section else []
    edges = [refs.pop(0) for _ in range(4)] if section else []
    q_win, n_win, buf_a, buf_b, coef, sems = refs
    members, window, lon = q_win.shape
    height = size * plan.tile
    base = place[section] * height
    start = pl.multiple_of(jnp.clip(base - 8, 0, plan.rows - window), 8)
    copies = [
        pltpu.make_async_copy(numbers.at[:, pl.ds(start, window), :], n_win, sems.at[0]),
        pltpu.make_async_copy(q.at[:, pl.ds(start, window), :], q_win, sems.at[1]),
    ]
    for i, first in enumerate((0, plan.rows - 8)) if section else []:
        rows = pl.ds(first, 8)
        copies.append(pltpu.make_async_copy(q.at[:, rows, :], edges[2 * i], sems.at[2 + 2 * i]))
        copies.append(
            pltpu.make_async_copy(numbers.at[:, rows, :], edges[2 * i + 1], sems.at[3 + 2 * i])
        )
    for copy in copies:
        copy.start()
    copies[0].wait()
    for i, c in enumerate(coefficients([n_win[i] for i in range(3)])):
        coef[i, 8 : 8 + window, :] = c
    copies[1].wait()
    shift = base - 8 - start

    def turn(g):
        at = pl.multiple_of(jnp.clip(g * 8 + shift, 0, window - 8), 8)
        return jnp.swapaxes(q_win[:, pl.ds(at, 8), :], 0, 1)

    def some_turns(g, _):
        buf_a[pl.ds(g * 8 - 4, 8)] = turn(g)
        return 0

    groups = height // 8 + 2
    buf_a[0:4] = turn(0)[4:]
    lax.fori_loop(1, groups - 1, some_turns, 0)
    buf_a[height + 4 : height + 8] = turn(groups - 1)[:4]
    src, dst = buf_a, buf_b
    for s in range(STEPS):
        step_rows(src, dst, coef, s + 1, height + 7 - s, shift + 12)
        src, dst = dst, src
    for i in range(size):
        r = section * size + i
        first = STEPS + (place[section] * size ^ r ^ place[plan.sections]) % size * plan.tile
        for slot, row in enumerate(plan.early):
            early[i][slot] = src[first + row]
        for slot, row in enumerate(plan.late):
            kept[i, slot] = src[first + row]
    for copy in copies[2:]:
        copy.wait()
    for side in range(2) if section else []:
        first = 0 if side == 0 else 8 - STEPS
        fields, stencil = edges[2 * side : 2 * side + 2]
        turned = jnp.swapaxes(fields[...], 0, 1)
        for row in range(STEPS):
            halos[side][row, :members] = turned[first + row]
            halos[side][row, members:] = jnp.zeros_like(halos[side][row, members:])
            for i in range(3):
                halos[side][row, members + i : members + i + 1] = stencil[
                    i, first + row : first + row + 1
                ]


def border_kernel(plan, place, low, high, q, numbers, *refs):
    kept = refs[: plan.sections]
    late = refs[plan.sections : plan.sections + plan.count]
    q_edge, n_edge, buf_a, buf_b, coef, final, sems = refs[plan.sections + plan.count :]
    me = place[plan.sections]
    members = q_edge.shape[1]
    wide = 3 * STEPS
    copies = []
    for side, first in enumerate((0, plan.rows - 2 * STEPS)):
        rows = pl.ds(first, 2 * STEPS)
        copies += [
            pltpu.make_async_copy(q.at[:, rows, :], q_edge.at[side], sems.at[2 * side]),
            pltpu.make_async_copy(numbers.at[:, rows, :], n_edge.at[side], sems.at[2 * side + 1]),
        ]
    for copy in copies:
        copy.start()
    for section in range(plan.sections):
        final[section * plan.size : (section + 1) * plan.size] = kept[section][...]
    for copy in copies:
        copy.wait()
    for side, halo in enumerate((low, high)):
        halo_at, own_at = (0, STEPS) if side == 0 else (2 * STEPS, 0)
        buf_a[halo_at : halo_at + STEPS] = halo[:, :members, :]
        buf_a[own_at : own_at + 2 * STEPS] = jnp.swapaxes(q_edge[side], 0, 1)
        halo_numbers = [halo[:, members + i, :] for i in range(3)]
        own_numbers = [n_edge[side, i] for i in range(3)]
        for i, (h, o) in enumerate(zip(coefficients(halo_numbers), coefficients(own_numbers))):
            coef[i, halo_at : halo_at + STEPS, :] = h
            coef[i, own_at : own_at + 2 * STEPS, :] = o
        src, dst = buf_a, buf_b
        for s in range(STEPS):
            step_rows(src, dst, coef, s + 1, wide - s - 1, 0)
            src, dst = dst, src
        for r in range(STEPS):
            row = r if side == 0 else plan.rows - STEPS + r
            final[me ^ (row // plan.tile), plan.late.index(row % plan.tile)] = src[STEPS + r]
    for r in range(plan.count):
        late[r][...] = final[r]


def split(x):
    high = x.astype(bf16)
    return high, (x - high.astype(f32)).astype(bf16)


def mm(a, b, dims=((1,), (0,))):
    return lax.dot_general(a, b, (dims, ((), ())), preferred_element_type=f32)


def analysis_kernel(plan, arrived, fresh, old_mix, old_fields, out_rows, keep_fields, *refs):
    refs = list(refs)
    count = plan.count
    take = lambda n: [refs.pop(0) for _ in range(n)]
    place, fresh_of, out_of = take(3)
    me = place[plan.sections]
    pieces = take(count) if arrived else []
    inn, prec, cells = take(3) if fresh else (None, None, None)
    weights = take(1)[0] if out_rows else None
    old_mix_refs = take(len(old_mix))
    old_field_refs = take(len(old_fields))
    mix_out = take(1)[0] if fresh else None
    kept_out = take(1)[0] if keep_fields else None
    outs = take(count) if out_rows else []
    mix, fields = take(2)
    tile = plan.tile
    members, lon = fields.shape[1:]
    share = members // count
    group = LANES // OB
    pack = plan.pack
    per_row = lon // LANES
    pairs = per_row // pack
    for slots, ref in zip(old_mix, old_mix_refs):
        for row, slot in slots:
            mix[row + 1] = ref[slot]
    for slots, ref in zip(old_fields, old_field_refs):
        for row, slot in slots:
            fields[row] = ref[slot]
    if arrived:
        for r in range(count):
            first = pl.multiple_of((me ^ r) * share, share)
            for slot, row in enumerate(arrived):
                fields[row, pl.ds(first, share), :] = pieces[r][slot]
    if fresh:

        def observe(slot, _):
            row = fresh_of[slot]
            for q in range(per_row // group):
                anomalies = []
                for t in range(group):
                    lanes = slice((q * group + t) * LANES, (q * group + t + 1) * LANES)
                    block = fields[row, :, lanes]
                    anomalies.append(block - jnp.mean(block, axis=0, keepdims=True))
                high, low = split(jnp.concatenate(anomalies, axis=0))
                at = row * (per_row // group) + q
                cell_row = cells[pl.ds(at, 1), :]
                chosen = (
                    lax.broadcasted_iota(jnp.int32, (LANES, LANES), 0)
                    == jnp.broadcast_to(cell_row, (LANES, LANES))
                )
                pick = jnp.where(chosen, 1.0, 0.0).astype(bf16)
                seen = mm(high, pick) + mm(low, pick)
                shape = seen.shape
                same = (
                    lax.broadcasted_iota(jnp.int32, shape, 0) // members
                    == lax.broadcasted_iota(jnp.int32, shape, 1) // OB
                )
                seen_high, seen_low = split(jnp.where(same, seen, 0.0))
                lanes = pl.ds(pl.multiple_of(at * LANES, LANES), LANES)
                weighted = inn[:, lanes] * prec[:, lanes]
                w_high, w_low = split(weighted)
                both = mm(
                    jnp.concatenate([w_high, w_low], axis=0), seen_high, ((1,), (1,))
                )
                total = both[:members] + both[members:] + mm(w_high, seen_low, ((1,), (1,)))
                wide = pack * members
                for k in range(group // pack):
                    mix[row + 1, q * (group // pack) + k] = total[:, k * wide : (k + 1) * wide]
            return 0

        lax.fori_loop(0, len(fresh), observe, 0)
        for slot, row in enumerate(fresh):
            mix_out[slot] = mix[row + 1]
    for slot, row in enumerate(keep_fields):
        kept_out[slot] = fields[row]
    if out_rows:
        reach = ceil_div(R, pack)
        width = 2 * reach + 1

        def update(slot, _):
            row = out_of[slot]
            for pair in range(pairs):
                sums = [jnp.zeros((members, pack * members), f32) for _ in range(pack)]
                for d in range(width):
                    place = pair + d - reach
                    step = place // pairs
                    part = mix[row + 1 + step, place - step * pairs]
                    for t in range(pack):
                        block = row * per_row + pair * pack + t
                        w = weights[block, pl.ds(d, 1), :]
                        sums[t] += part * jnp.broadcast_to(w, part.shape)
                for t in range(pack):
                    first = (pair * pack + t) * LANES
                    cells_here = fields[row, :, first : first + LANES]
                    anomaly = cells_here - jnp.mean(cells_here, axis=0, keepdims=True)
                    a_high, a_low = split(anomaly)
                    a_high = jnp.concatenate([a_high] * pack, axis=0)
                    a_low = jnp.concatenate([a_low] * pack, axis=0)
                    s_high, s_low = split(sums[t])
                    both = mm(jnp.concatenate([s_high, s_low], axis=0), a_high)
                    done = cells_here + both[:members] + both[members:] + mm(s_high, a_low)
                    fields[row, :, first : first + LANES] = done
            return 0

        lax.fori_loop(0, len(out_rows), update, 0)
        for r in range(count):
            first = pl.multiple_of((me ^ r) * share, share)
            for slot, row in enumerate(out_rows):
                outs[r][slot] = fields[row, pl.ds(first, share), :]


def assemble_kernel(plan, parts, place, *refs):
    pieces, (out, buf) = refs[:-2], refs[-2:]
    me = place[plan.sections]
    at = 0
    for rows in parts:
        for r in range(plan.count):
            base = (me ^ r) * plan.tile
            for slot, row in enumerate(rows):
                buf[base + row] = pieces[at + r][slot]
        at += plan.count

    def turn(g, _):
        r = pl.multiple_of(g * 8, 8)
        out[:, pl.ds(r, 8), :] = jnp.swapaxes(buf[pl.ds(r, 8)], 0, 1)
        return 0

    lax.fori_loop(0, plan.rows // 8, turn, 0)


class Plan:
    def __init__(self, rows, count, members, sections):
        assert count >= 4 and count & (count - 1) == 0
        self.rows = rows
        self.count = count
        self.sections = sections
        self.size = count // self.sections
        self.tile = rows // count
        self.pack = max(1, LANES // members)
        self.early = [r for r in range(self.tile) if STEPS <= r < self.tile - STEPS]
        self.late = [r for r in range(self.tile) if r not in self.early]


def shards(initial, stencil_numbers, innovations, obs_prec, obs_cell, band_idx):
    share, rows, lon = initial.shape
    count = lax.axis_size("member")
    members = share * count
    plan = Plan(rows, count, members, SECTIONS)
    tile, pack, size = plan.tile, plan.pack, plan.size
    per_row = lon // LANES
    pairs = per_row // pack
    me = lax.axis_index("member")
    place = jnp.stack([me // size ^ i for i in range(plan.sections)] + [me]).astype(jnp.int32)
    sds = lambda *shape: jax.ShapeDtypeStruct(shape, f32)
    ints = lambda values: jnp.array(list(values) or [0], jnp.int32)

    early_rows, late_rows = len(plan.early), len(plan.late)
    height = size * tile
    window = min(rows, height + (8 if plan.sections == 2 else 16))
    chain = Chain(FLIGHT)
    half = count // 2
    far, near = list(reversed(range(half, count))), list(reversed(range(1, half)))
    turns = far[:2]
    for i in range(half):
        turns += near[i : i + 1] + far[i + 2 : i + 3]

    def send(pieces, partners, *earlier):
        got = list(pieces)
        for r in partners:
            piece = after(pieces[r], *earlier) if earlier and r == partners[-1] else pieces[r]
            got[r] = chain.swap(piece, r)
        return got

    def forecast(section, order):
        shapes = []
        if plan.early:
            shapes = [sds(early_rows, share, lon)] * size
        shapes.append(sds(size, late_rows, share, lon))
        scratch = []
        if section:
            shapes += [sds(STEPS, share + 8, lon)] * 2
            scratch = [pltpu.VMEM((share, 8, lon), f32), pltpu.VMEM((3, 8, lon), f32)] * 2
        return pl.pallas_call(
            functools.partial(section_kernel, plan, section),
            out_shape=shapes,
            in_specs=[SMEM, HBM, HBM],
            out_specs=[VMEM] * len(shapes),
            scratch_shapes=scratch
            + [
                pltpu.VMEM((share, window, lon), f32),
                pltpu.VMEM((3, window, lon), f32),
                pltpu.VMEM((height + 8, share, lon), f32),
                pltpu.VMEM((height + 8, share, lon), f32),
                pltpu.VMEM((5, window + 16, lon), f32),
                pltpu.SemaphoreType.DMA((6,)),
            ],
            compiler_params=params(SECTION_MIB),
            cost_estimate=hint(9),
            name=f"section_{section}",
        )(order, initial, stencil_numbers)

    far_outs = forecast(1, place)
    near_outs = forecast(0, after(place, far_outs[-1]))
    kept_far, kept_near = far_outs[-3], near_outs[-1]
    if plan.early:
        early = near_outs[:size] + far_outs[:size]
        low = chain.shift(far_outs[-1], "slab", 1)
        early = send(early, far[:2])
        high = chain.shift(far_outs[-2], "slab", -1)
        early = send(early, far[2:3] + [r for r in turns[2:] if r != far[2]])
    else:
        low = chain.shift(far_outs[-1], "slab", 1)
        high = chain.shift(far_outs[-2], "slab", -1)
    late = pl.pallas_call(
        functools.partial(border_kernel, plan),
        out_shape=[sds(late_rows, share, lon)] * count,
        in_specs=[SMEM, VMEM, VMEM, HBM, HBM] + [VMEM] * plan.sections,
        out_specs=[VMEM] * count,
        scratch_shapes=[
            pltpu.VMEM((2, share, 2 * STEPS, lon), f32),
            pltpu.VMEM((2, 3, 2 * STEPS, lon), f32),
            pltpu.VMEM((3 * STEPS, share, lon), f32),
            pltpu.VMEM((3 * STEPS, share, lon), f32),
            pltpu.VMEM((5, 3 * STEPS, lon), f32),
            pltpu.VMEM((count, late_rows, share, lon), f32),
            pltpu.SemaphoreType.DMA((4,)),
        ],
        compiler_params=params(BORDER_MIB),
        cost_estimate=hint(4),
        name="border",
    )(place, low, high, initial, stencil_numbers, kept_near, kept_far)

    blocks = tile * per_row
    first_block = lax.axis_index(("slab", "member")) * blocks
    own = first_block + jnp.arange(blocks, dtype=jnp.int32)
    reach = ceil_div(R, pack)
    width = 2 * reach + 1
    start = own // pack * pack - reach * pack
    reached = start[:, None] + jnp.arange(width * pack, dtype=jnp.int32)
    in_band = jnp.any(reached[:, :, None] == band_idx[:, None, :], axis=2)
    distance = jnp.abs(reached - own[:, None]).astype(f32)
    tapers = jnp.where(in_band, 1.0 - distance / (R + 1.0), 0.0) / (members - 1)
    weights = jnp.repeat(tapers, members, axis=1).reshape(blocks, width, pack * members)
    prec = obs_prec.reshape(1, -1)
    cells = obs_cell.reshape(-1, LANES)

    def analyse(arrived, pieces, fresh, old_mix, old_fields, out_rows, keep_fields, name, order=place):
        args = [order, ints(fresh), ints(out_rows)]
        shapes = []
        if arrived:
            args += pieces
        if fresh:
            args += [innovations, prec, cells]
            shapes += [sds(len(fresh), pairs, members, pack * members)]
        if out_rows:
            args += [weights]
        args += [m[1] for m in old_mix] + [f[1] for f in old_fields]
        if keep_fields:
            shapes += [sds(len(keep_fields), members, lon)]
        if out_rows:
            shapes += [sds(len(out_rows), share, lon)] * count
        made = list(
            pl.pallas_call(
                functools.partial(
                    analysis_kernel,
                    plan,
                    arrived,
                    fresh,
                    [m[0] for m in old_mix],
                    [f[0] for f in old_fields],
                    out_rows,
                    keep_fields,
                ),
                out_shape=shapes,
                in_specs=[SMEM] * 3 + [VMEM] * (len(args) - 3),
                out_specs=[VMEM] * len(shapes),
                scratch_shapes=[
                    pltpu.VMEM((tile + 2, pairs, members, pack * members), f32),
                    pltpu.VMEM((tile, members, lon), f32),
                ],
                compiler_params=params(ANALYSIS_MIB),
                cost_estimate=hint(0 if name in SHORT else 1.2 * len(fresh)),
                name=name,
            )(*args)
        )
        mixing = made.pop(0) if fresh else None
        fields = made.pop(0) if keep_fields else None
        return mixing, fields, made

    slots = lambda rows: [(row, slot) for slot, row in enumerate(rows)]
    parts, returned = [], []
    inner = [r for r in plan.early if r - 1 in plan.early and r + 1 in plan.early]
    old_mix, old_fields, order = [], [], place
    if plan.early:
        edge = [r for r in plan.early if r not in inner]
        mixing, fields, back = analyse(
            plan.early, early, plan.early, [], [], inner, edge, "analyse_early"
        )
        old_mix = [(slots(plan.early), mixing)]
        old_fields = [(slots(edge), fields)] if edge else []
        late = send(late, turns, fields if edge else mixing)
        order = after(place, mixing)
        if inner:
            parts.append(inner)
            back = send(back, far[:2])
    else:
        late = send(late, turns)
    rims = sorted({0, tile - 1})
    rest = [r for r in plan.late if r not in rims]
    mixing, _, _ = analyse(plan.late, late, rims, [], [], [], [], "mix_rims", order)
    axes = ("slab", "member")
    from_prev = chain.shift(mixing[rims.index(tile - 1)][None], axes, 1)
    from_next = chain.shift(mixing[0][None], axes, -1)
    if inner:
        returned += send(back, far[2:] + near)
    old_mix += [(slots(rims), mixing), ([(-1, 0)], from_prev), ([(tile, 0)], from_next)]
    if rest:
        mixing, _, _ = analyse(plan.late, late, rest, [], [], [], [], "mix_late", after(place, mixing))
        old_mix += [(slots(rest), mixing)]
    others = [r for r in range(tile) if r not in inner]
    _, _, back = analyse(plan.late, late, [], old_mix, old_fields, others, [], "analyse_late")
    parts.append(others)
    returned += send(back, turns)

    return pl.pallas_call(
        functools.partial(assemble_kernel, plan, parts),
        out_shape=sds(share, rows, lon),
        in_specs=[SMEM] + [VMEM] * len(returned),
        out_specs=VMEM,
        scratch_shapes=[pltpu.VMEM((rows, share, lon), f32)],
        compiler_params=params(32),
        cost_estimate=hint(4),
        name="assemble",
    )(place, *returned)


def solution(mesh):
    in_specs = (
        P("member", "slab", None),
        P(None, "slab", None),
        P(None, ("slab", "member")),
        P(("slab", "member")),
        P(("slab", "member"), None),
        P(("slab", "member"), None),
    )
    out_specs = P("member", "slab", None)
    return jax.shard_map(shards, mesh=mesh, in_specs=in_specs, out_specs=out_specs, check_vma=False)
```

time: 253 us -> 218 us (0.86)
  the two profiles are of different devices: /device:TPU:11 before, /device:TPU:0 now
where the time goes in v2:
time: 218 us
  starting transfers between devices  76 us (35%)
  waiting for transfers between devices  69.4 us (32%)
  Pallas kernels  56.7 us (26%)
  local copies, waits for them, and re-layouts  14 us (6%)
    ppermute x32, starting transfers between devices, permute(): self.ended.append(lax.ppermute(piece, axis, route))  76 us
    ppermute x32, waiting for transfers between devices, permute(): self.ended.append(lax.ppermute(piece, axis, route))  69.4 us
    pallas_call x4, Pallas kernels, analyse(): pl.pallas_call(functools.partial(analysis_kernel, plan, arrived, fresh, [...  28.2 us
    pallas_call x2, Pallas kernels, forecast(): pl.pallas_call(functools.partial(section_kernel, plan, section), out_shap...  21.9 us
    unnamed x63, local copies, waits for them, and re-layouts  11 us
  transfers between devices with their start and end apart: 32, of which 8 were waited for; matrix products, arithmetic and copies ran while one was open for 2% of the time, Pallas kernels for 19%

profile of v2, /device:TPU:0, one launch (start us, length us, event | category | flops | bytes accessed | tf_op | source)
XLA Modules:
  0.0 217.6 jit_solution(14500338124597935459)
XLA Ops:
  0.6 11.0 %section_1.1 = (f32[8,8,1024]{2,1,0:T(8,128)}, f32[8,8,1024]{2,1,0:T(8,128)}, f32[8,8,1024]{2,1,0:T(8,128)}, f32[8,8,1024]{2,1,0:T(8,128)}, f32[4,8,8,1024]{3,2,...) custom-call(s32[3]{0:T(128)} %pad_add_fusion.place.refs_0_, f32[8,128,1024]{2,1,0:T(8,128)} %q.5, ...), custom_call_target="tpu_custom_call" | custom-call | bytes 33210000 | tf_op jit(solution)/shard_map/section_1/pallas_call | solution.py:397
  11.6 5.0 %collective-permute-start.4 = (f32[4,16,1024]{2,1,0:T(8,128)}, f32[4,16,1024]{2,1,0:T(8,128)S(1)}, u32[]{:S(2)}, u32[]{:S(2)}) collective-permute-start(f32[4,16,1024]{2,1,0:T(8,128)} %get-tuple-element.74), channel_id=1, source_target_pairs={{0,8},{8,16},{16,24},{1,9},{9,17},{17,25},{2,10},{10,18},{18,26},{... | collective-permute-start | bytes 786440 | tf_op jit(solution)/shard_map/ppermute | solution.py:52
  16.6 2.8 %collective-permute-start.2 = (f32[8,8,1024]{2,1,0:T(8,128)}, f32[8,8,1024]{2,1,0:T(8,128)S(1)}, u32[]{:S(2)}, u32[]{:S(2)}) collective-permute-start(f32[8,8,1024]{2,1,0:T(8,128)} %get-tuple-element.81), channel_id=1, source_target_pairs={{0,7},{1,6},{2,5},{3,4},{4,3},{5,2},{6,1},{7,0},{8,15},{9,14},{10,... | collective-permute-start | bytes 786440 | tf_op jit(solution)/shard_map/ppermute | solution.py:52
  22.1 10.9 %section_0.1 = (f32[8,8,1024]{2,1,0:T(8,128)}, f32[8,8,1024]{2,1,0:T(8,128)}, f32[8,8,1024]{2,1,0:T(8,128)}, f32[8,8,1024]{2,1,0:T(8,128)}, f32[4,8,8,1024]{3,2,1,0:T(8,128)}) custom-call(s32[3]{0:T(128)} %pad_add_fusion.place.refs_0_, f32[8,128,1024]{2,1,0:T(8,128)} %q.5, f32[3,128,1024]{2,1,0:T(8,128)} %numbers.5), custom_call_target="tpu_custom_call" | custom-call | bytes 33210000 | tf_op jit(solution)/shard_map/section_0/pallas_call | solution.py:397
  33.0 2.9 %collective-permute-start.5 = (f32[8,8,1024]{2,1,0:T(8,128)}, f32[8,8,1024]{2,1,0:T(8,128)S(1)}, u32[]{:S(2)}, u32[]{:S(2)}) collective-permute-start(f32[8,8,1024]{2,1,0:T(8,128)} %get-tuple-element.84), channel_id=1, source_target_pairs={{0,3},{1,2},{2,1},{3,0},{4,7},{5,6},{6,5},{7,4},{8,11},{9,10},{10,... | collective-permute-start | bytes 786440 | tf_op jit(solution)/shard_map/ppermute | solution.py:52
  35.9 7.9 %collective-permute-start.3 = (f32[8,8,1024]{2,1,0:T(8,128)}, f32[8,8,1024]{2,1,0:T(8,128)}, u32[]{:S(2)}, u32[]{:S(2)}) collective-permute-start(f32[8,8,1024]{2,1,0:T(8,128)} %get-tuple-element.82), channel_id=1, source_target_pairs={{0,2},{1,3},{2,0},{3,1},{4,6},{5,7},{6,4},{7,5},{8,10},{9,11},{10,... | collective-permute-start | bytes 786440 | tf_op jit(solution)/shard_map/ppermute | solution.py:52
  43.8 6.3 %collective-permute-start.7 = (f32[8,8,1024]{2,1,0:T(8,128)}, f32[8,8,1024]{2,1,0:T(8,128)}, u32[]{:S(2)}, u32[]{:S(2)}) collective-permute-start(f32[8,8,1024]{2,1,0:T(8,128)} %get-tuple-element.87), channel_id=1, source_target_pairs={{0,4},{1,5},{2,6},{3,7},{4,0},{5,1},{6,2},{7,3},{8,12},{9,13},{10,... | collective-permute-start | bytes 786440 | tf_op jit(solution)/shard_map/ppermute | solution.py:52
  50.5 2.2 %copy-done = f32[8,128,1024]{2,1,0:T(8,128)S(1)} copy-done((f32[8,128,1024]{2,1,0:T(8,128)S(1)}, f32[8,128,1024]{2,1,0:T(8,128)}, u32[]{:S(2)}) %copy-start) | copy-done | bytes 4194328
  53.9 3.0 %border.1 = (f32[8,8,1024]{2,1,0:T(8,128)S(1)}, f32[8,8,1024]{2,1,0:T(8,128)S(1)}, f32[8,8,1024]{2,1,0:T(8,128)S(1)}, f32[8,8,1024]{2,1,0:T(8,128)S(1)}, f32[8,8...) custom-call(s32[3]{0:T(128)S(1)} %copy-done.7, ...), custom_call_target="tpu_custom_call" | custom-call | bytes 14760000 | tf_op jit(solution)/shard_map/border/pallas_call | solution.py:428
  60.5 1.8 collective-permute-start.13
  63.0 1.8 collective-permute-start.9
  67.0 10.3 %collective-permute-done.7.refs_7_ = f32[8,8,1024]{2,1,0:T(8,128)} collective-permute-done((f32[8,8,1024]{2,1,0:T(8,128)}, f32[8,8,1024]{2,1,0:T(8,128)}, u32[]{:S(2)}, u32[]{:S(2)}) %collective-permute-start.7) | collective-permute-done | bytes 262176 | tf_op jit(solution)/shard_map/ppermute | solution.py:52
  77.4 10.1 %analyse_early.1 = (f32[8,4,64,128]{3,2,1,0:T(8,128)}, f32[2,64,1024]{2,1,0:T(8,128)}, f32[6,8,1024]{2,1,0:T(8,128)}, f32[6,8,1024]{2,1,0:T(8,128)}, f32[6,8,102...) custom-call(s32[3]{0:T(128)} %pad_add_fusion.place.refs_0_, ...), custom_call_target="tpu_custom_call" | custom-call | bytes 35424000 | tf_op jit(solution)/shard_map/analyse_early/pallas_call | solution.py:477
  87.6 7.9 %collective-permute-start.14 = (f32[8,8,1024]{2,1,0:T(8,128)S(1)}, f32[8,8,1024]{2,1,0:T(8,128)S(1)}, u32[]{:S(2)}, u32[]{:S(2)}) collective-permute-start(f32[8,8,1024]{2,1,0:T(8,128)S(1)} %copy-done.10), channel_id=1, source_target_pairs={{0,4},{1,5},{2,6},{3,7},{4,0},{5,1},{6,2},{7,3},{8,12},{9,13},{10,... | collective-permute-start | bytes 786440 | tf_op jit(solution)/shard_map/ppermute | solution.py:52
  97.6 15.8 %collective-permute-done.22.refs_7_ = f32[6,8,1024]{2,1,0:T(8,128)S(1)} collective-permute-done((f32[6,8,1024]{2,1,0:T(8,128)}, f32[6,8,1024]{2,1,0:T(8,128)S(1)}, u32[]{:S(2)}, u32[]{:S(2)}) %collective-permute-start.22) | collective-permute-done | bytes 196640 | tf_op jit(solution)/shard_map/ppermute | solution.py:52
  113.4 7.2 %collective-permute-start.23 = (f32[6,8,1024]{2,1,0:T(8,128)}, f32[6,8,1024]{2,1,0:T(8,128)S(1)}, u32[]{:S(2)}, u32[]{:S(2)}) collective-permute-start(f32[6,8,1024]{2,1,0:T(8,128)} %get-tuple-element.124), channel_id=1, source_target_pairs={{0,4},{1,5},{2,6},{3,7},{4,0},{5,1},{6,2},{7,3},{8,12},{9,13},{10,... | collective-permute-start | bytes 589832 | tf_op jit(solution)/shard_map/ppermute | solution.py:52
  121.6 3.7 %mix_rims.1.refs_13_ = f32[2,4,64,128]{3,2,1,0:T(8,128)} custom-call(s32[3]{0:T(128)} %pad_add_fusion.place.refs_0_, s32[2]{0:T(128)} %iota_multiply_fusion.refs_1_, s32[1]{0:T(128)} %constant.74.clone.refs_2_.refs_1_, f32[8,8,1024]{2,1,0:T(8,128)} %copy-done.2, f32[8,8,1024]{2,1,0:T(8,128)} %copy-done.19, f32[8,8,1024]{2,1,0:T(8,128)} %copy-done.21, ...), custom_call_target="tpu_custom_call" | custom-call | tf_op jit(solution)/shard_map/mix_rims/pallas_call | solution.py:477
  127.6 3.2 %collective-permute-start.18 = (f32[1,4,64,128]{3,2,1,0:T(8,128)S(1)}, f32[1,4,64,128]{3,2,1,0:T(8,128)S(1)}, u32[]{:S(2)}, u32[]{:S(2)}) collective-permute-start(f32[1,4,64,128]{3,2,1,0:T(8,128)S(1)} %get-tuple-element.115), channel_id=1, source_target_pairs={{0,1},{1,2},{2,3},{3,4},{4,5},{5,6},{6,7},{7,8},{8,9},{9,10},{10,1... | collective-permute-start | bytes 393224 | tf_op jit(solution)/shard_map/ppermute | solution.py:52
  130.9 3.6 %collective-permute-start.20 = (f32[6,8,1024]{2,1,0:T(8,128)}, f32[6,8,1024]{2,1,0:T(8,128)S(1)}, u32[]{:S(2)}, u32[]{:S(2)}) collective-permute-start(f32[6,8,1024]{2,1,0:T(8,128)} %get-tuple-element.119), channel_id=1, source_target_pairs={{0,6},{1,7},{2,4},{3,5},{4,2},{5,3},{6,0},{7,1},{8,14},{9,15},{10,... | collective-permute-start | bytes 589832 | tf_op jit(solution)/shard_map/ppermute | solution.py:52
  134.4 5.8 %mix_late.1.refs_16_ = f32[6,4,64,128]{3,2,1,0:T(8,128)} custom-call(s32[3]{0:T(128)} %pad_add_fusion.place.refs_0_, s32[6]{0:T(128)} %constant.75.clone.refs_1_, s32[1]{0:T(128)} %constant.74.clone.refs_2_.refs_1_, f32[8,8,1024]{2,1,0:T(8,128)} %copy-done.2, f32[8,8,1024]{2,1,0:T(8,128)} %copy-done.19, f32[8,8,1024]{2,1,0:T(8,128)} %copy-done.21, ...), custom_call_target="tpu_custom_call" | custom-call | tf_op jit(solution)/shard_map/mix_late/pallas_call | solution.py:477
  141.5 8.6 %analyse_late.1 = (f32[10,8,1024]{2,1,0:T(8,128)}, f32[10,8,1024]{2,1,0:T(8,128)}, f32[10,8,1024]{2,1,0:T(8,128)}, f32[10,8,1024]{2,1,0:T(8,128)}, f32[10,8,1024...) custom-call(s32[3]{0:T(128)} %pad_add_fusion.place.refs_0_, ...), custom_call_target="tpu_custom_call" | custom-call | tf_op jit(solution)/shard_map/analyse_late/pallas_call | solution.py:477
  150.1 4.9 %collective-permute-start.25 = (f32[10,8,1024]{2,1,0:T(8,128)}, f32[10,8,1024]{2,1,0:T(8,128)S(1)}, u32[]{:S(2)}, u32[]{:S(2)}) collective-permute-start(f32[10,8,1024]{2,1,0:T(8,128)} %get-tuple-element.131), channel_id=1, source_target_pairs={{0,6},{1,7},{2,4},{3,5},{4,2},{5,3},{6,0},{7,1},{8,14},{9,15},{10,... | collective-permute-start | bytes 983048 | tf_op jit(solution)/shard_map/ppermute | solution.py:52
  155.1 3.2 %collective-permute-start.29 = (f32[10,8,1024]{2,1,0:T(8,128)}, f32[10,8,1024]{2,1,0:T(8,128)S(1)}, u32[]{:S(2)}, u32[]{:S(2)}) collective-permute-start(f32[10,8,1024]{2,1,0:T(8,128)} %get-tuple-element.139), channel_id=1, source_target_pairs={{0,7},{1,6},{2,5},{3,4},{4,3},{5,2},{6,1},{7,0},{8,15},{9,14},{10,... | collective-permute-start | bytes 983048 | tf_op jit(solution)/shard_map/ppermute | solution.py:52
  160.4 14.8 %collective-permute-done.21.refs_3_ = f32[6,8,1024]{2,1,0:T(8,128)S(1)} collective-permute-done((f32[6,8,1024]{2,1,0:T(8,128)S(1)}, f32[6,8,1024]{2,1,0:T(8,128)S(1)}, u32[]{:S(2)}, u32[]{:S(2)}) %collective-permute-start.21) | collective-permute-done | bytes 196640 | tf_op jit(solution)/shard_map/ppermute | solution.py:52
  175.2 1.6 collective-permute-start.28
  176.8 2.5 %collective-permute-done.19.refs_2_ = f32[6,8,1024]{2,1,0:T(8,128)S(1)} collective-permute-done((f32[6,8,1024]{2,1,0:T(8,128)S(1)}, f32[6,8,1024]{2,1,0:T(8,128)S(1)}, u32[]{:S(2)}, u32[]{:S(2)}) %collective-permute-start.19) | collective-permute-done | bytes 196640 | tf_op jit(solution)/shard_map/ppermute | solution.py:52
  180.2 2.5 %collective-permute-start.27 = (f32[10,8,1024]{2,1,0:T(8,128)}, f32[10,8,1024]{2,1,0:T(8,128)S(1)}, u32[]{:S(2)}, u32[]{:S(2)}) collective-permute-start(f32[10,8,1024]{2,1,0:T(8,128)} %get-tuple-element.134), channel_id=1, source_target_pairs={{0,2},{1,3},{2,0},{3,1},{4,6},{5,7},{6,4},{7,5},{8,10},{9,11},{10,... | collective-permute-start | bytes 983048 | tf_op jit(solution)/shard_map/ppermute | solution.py:52
  183.0 4.1 %collective-permute-start.30 = (f32[10,8,1024]{2,1,0:T(8,128)}, f32[10,8,1024]{2,1,0:T(8,128)S(1)}, u32[]{:S(2)}, u32[]{:S(2)}) collective-permute-start(f32[10,8,1024]{2,1,0:T(8,128)} %get-tuple-element.140), channel_id=1, source_target_pairs={{0,4},{1,5},{2,6},{3,7},{4,0},{5,1},{6,2},{7,3},{8,12},{9,13},{10,... | collective-permute-start | bytes 983048 | tf_op jit(solution)/shard_map/ppermute | solution.py:52
  188.6 10.6 %collective-permute-done.31.refs_13_ = f32[10,8,1024]{2,1,0:T(8,128)S(1)} collective-permute-done((f32[10,8,1024]{2,1,0:T(8,128)}, f32[10,8,1024]{2,1,0:T(8,128)S(1)}, u32[]{:S(2)}, u32[]{:S(2)}) %collective-permute-start.31) | collective-permute-done | bytes 327712 | tf_op jit(solution)/shard_map/ppermute | solution.py:52
  199.2 3.3 %collective-permute-done.27.refs_10_ = f32[10,8,1024]{2,1,0:T(8,128)S(1)} collective-permute-done((f32[10,8,1024]{2,1,0:T(8,128)}, f32[10,8,1024]{2,1,0:T(8,128)S(1)}, u32[]{:S(2)}, u32[]{:S(2)}) %collective-permute-start.27) | collective-permute-done | bytes 327712 | tf_op jit(solution)/shard_map/ppermute | solution.py:52
  202.5 10.5 %collective-permute-done.30.refs_12_ = f32[10,8,1024]{2,1,0:T(8,128)S(1)} collective-permute-done((f32[10,8,1024]{2,1,0:T(8,128)}, f32[10,8,1024]{2,1,0:T(8,128)S(1)}, u32[]{:S(2)}, u32[]{:S(2)}) %collective-permute-start.30) | collective-permute-done | bytes 327712 | tf_op jit(solution)/shard_map/ppermute | solution.py:52
  214.0 3.7 %assemble.1 = f32[8,128,1024]{2,1,0:T(8,128)} custom-call(s32[3]{0:T(128)S(1)} %copy-done.8, f32[6,8,1024]{2,1,0:T(8,128)S(1)} %copy-done.6, f32[6,8,1024]{2,1,0:T(8,128)S(1)} %collective-permute-done.17.refs_1_, f32[6,8,1024]{2,1,0:T(8,128)S(1)} %collective-permute-done.19.refs_2_, f32[6,8,1024]{2,1,0:T(8,128)S(1)} %collective-permute-done.21.refs_3_, ...), custom_call_target="tpu_custom_call" | custom-call | bytes 14760000 | tf_op jit(solution)/shard_map/assemble/pallas_call | solution.py:539
  (113 shorter events, 23.7 us)
Async XLA Ops:
  11.6 21.3 %collective-permute-start.4 = (f32[4,16,1024]{2,1,0:T(8,128)}, f32[4,16,1024]{2,1,0:T(8,128)S(1)}, u32[]{:S(2)}, u32[]{:S(2)}) collective-permute-start(f32[4,16,1024]{2,1,0:T(8,128)} %get-tuple-element.74), channel_id=1, source_target_pairs={{0,8},{8,16},{16,24},{1,9},{9,17},{17,25},{2,10},{10,18},{18,26},{... | collective-permute-start | bytes 786440 | tf_op jit(solution)/shard_map/ppermute | solution.py:52
  16.6 19.3 %collective-permute-start.2 = (f32[8,8,1024]{2,1,0:T(8,128)}, f32[8,8,1024]{2,1,0:T(8,128)S(1)}, u32[]{:S(2)}, u32[]{:S(2)}) collective-permute-start(f32[8,8,1024]{2,1,0:T(8,128)} %get-tuple-element.81), channel_id=1, source_target_pairs={{0,7},{1,6},{2,5},{3,4},{4,3},{5,2},{6,1},{7,0},{8,15},{9,14},{10,... | collective-permute-start | bytes 786440 | tf_op jit(solution)/shard_map/ppermute | solution.py:52
  19.4 30.7 %collective-permute-start = (f32[4,16,1024]{2,1,0:T(8,128)}, f32[4,16,1024]{2,1,0:T(8,128)S(1)}, u32[]{:S(2)}, u32[]{:S(2)}) collective-permute-start(f32[4,16,1024]{2,1,0:T(8,128)} %get-tuple-element.78), channel_id=1, source_target_pairs={{8,0},{16,8},{24,16},{9,1},{17,9},{25,17},{10,2},{18,10},{26,18},{... | collective-permute-start | bytes 786440 | tf_op jit(solution)/shard_map/ppermute | solution.py:52
  20.7 23.1 %collective-permute-start.6 = (f32[8,8,1024]{2,1,0:T(8,128)}, f32[8,8,1024]{2,1,0:T(8,128)}, u32[]{:S(2)}, u32[]{:S(2)}) collective-permute-start(f32[8,8,1024]{2,1,0:T(8,128)} %get-tuple-element.86), channel_id=1, source_target_pairs={{0,6},{1,7},{2,4},{3,5},{4,2},{5,3},{6,0},{7,1},{8,14},{9,15},{10,... | collective-permute-start | bytes 786440 | tf_op jit(solution)/shard_map/ppermute | solution.py:52
  21.7 38.8 %collective-permute-start.8 = (f32[8,8,1024]{2,1,0:T(8,128)}, f32[8,8,1024]{2,1,0:T(8,128)}, u32[]{:S(2)}, u32[]{:S(2)}) collective-permute-start(f32[8,8,1024]{2,1,0:T(8,128)} %get-tuple-element.88), channel_id=1, source_target_pairs={{0,5},{1,4},{2,7},{3,6},{4,1},{5,0},{6,3},{7,2},{8,13},{9,12},{10,... | collective-permute-start | bytes 786440 | tf_op jit(solution)/shard_map/ppermute | solution.py:52
  33.0 29.3 %collective-permute-start.5 = (f32[8,8,1024]{2,1,0:T(8,128)}, f32[8,8,1024]{2,1,0:T(8,128)S(1)}, u32[]{:S(2)}, u32[]{:S(2)}) collective-permute-start(f32[8,8,1024]{2,1,0:T(8,128)} %get-tuple-element.84), channel_id=1, source_target_pairs={{0,3},{1,2},{2,1},{3,0},{4,7},{5,6},{6,5},{7,4},{8,11},{9,10},{10,... | collective-permute-start | bytes 786440 | tf_op jit(solution)/shard_map/ppermute | solution.py:52
  35.9 29.7 %collective-permute-start.3 = (f32[8,8,1024]{2,1,0:T(8,128)}, f32[8,8,1024]{2,1,0:T(8,128)}, u32[]{:S(2)}, u32[]{:S(2)}) collective-permute-start(f32[8,8,1024]{2,1,0:T(8,128)} %get-tuple-element.82), channel_id=1, source_target_pairs={{0,2},{1,3},{2,0},{3,1},{4,6},{5,7},{6,4},{7,5},{8,10},{9,11},{10,... | collective-permute-start | bytes 786440 | tf_op jit(solution)/shard_map/ppermute | solution.py:52
  43.8 33.6 %collective-permute-start.7 = (f32[8,8,1024]{2,1,0:T(8,128)}, f32[8,8,1024]{2,1,0:T(8,128)}, u32[]{:S(2)}, u32[]{:S(2)}) collective-permute-start(f32[8,8,1024]{2,1,0:T(8,128)} %get-tuple-element.87), channel_id=1, source_target_pairs={{0,4},{1,5},{2,6},{3,7},{4,0},{5,1},{6,2},{7,3},{8,12},{9,13},{10,... | collective-permute-start | bytes 786440 | tf_op jit(solution)/shard_map/ppermute | solution.py:52
  50.1 16.9 %collective-permute-start.1 = (f32[8,8,1024]{2,1,0:T(8,128)}, f32[8,8,1024]{2,1,0:T(8,128)}, u32[]{:S(2)}, u32[]{:S(2)}) collective-permute-start(f32[8,8,1024]{2,1,0:T(8,128)} %get-tuple-element.79), channel_id=1, source_target_pairs={{0,1},{1,0},{2,3},{3,2},{4,5},{5,4},{6,7},{7,6},{8,9},{9,8},{10,11... | collective-permute-start | bytes 786440 | tf_op jit(solution)/shard_map/ppermute | solution.py:52
  60.5 27.1 %collective-permute-start.13 = (f32[8,8,1024]{2,1,0:T(8,128)}, f32[8,8,1024]{2,1,0:T(8,128)S(1)}, u32[]{:S(2)}, u32[]{:S(2)}) collective-permute-start(f32[8,8,1024]{2,1,0:T(8,128)} %get-tuple-element.108), channel_id=1, source_target_pairs={{0,7},{1,6},{2,5},{3,4},{4,3},{5,2},{6,1},{7,0},{8,15},{9,14},{10,... | collective-permute-start | bytes 786440 | tf_op jit(solution)/shard_map/ppermute | solution.py:52
  63.0 24.5 %collective-permute-start.9 = (f32[8,8,1024]{2,1,0:T(8,128)}, f32[8,8,1024]{2,1,0:T(8,128)S(1)}, u32[]{:S(2)}, u32[]{:S(2)}) collective-permute-start(f32[8,8,1024]{2,1,0:T(8,128)} %get-tuple-element.100), channel_id=1, source_target_pairs={{0,6},{1,7},{2,4},{3,5},{4,2},{5,3},{6,0},{7,1},{8,14},{9,15},{10,... | collective-permute-start | bytes 786440 | tf_op jit(solution)/shard_map/ppermute | solution.py:52
  65.6 29.9 %collective-permute-start.12 = (f32[8,8,1024]{2,1,0:T(8,128)}, f32[8,8,1024]{2,1,0:T(8,128)S(1)}, u32[]{:S(2)}, u32[]{:S(2)}) collective-permute-start(f32[8,8,1024]{2,1,0:T(8,128)} %copy-done.14), channel_id=1, source_target_pairs={{0,3},{1,2},{2,1},{3,0},{4,7},{5,6},{6,5},{7,4},{8,11},{9,10},{10,... | collective-permute-start | bytes 786440 | tf_op jit(solution)/shard_map/ppermute | solution.py:52
  77.4 43.2 %collective-permute-start.15 = (f32[8,8,1024]{2,1,0:T(8,128)}, f32[8,8,1024]{2,1,0:T(8,128)S(1)}, u32[]{:S(2)}, u32[]{:S(2)}) collective-permute-start(f32[8,8,1024]{2,1,0:T(8,128)} %copy-done.11), channel_id=1, source_target_pairs={{0,5},{1,4},{2,7},{3,6},{4,1},{5,0},{6,3},{7,2},{8,13},{9,12},{10,... | collective-permute-start | bytes 786440 | tf_op jit(solution)/shard_map/ppermute | solution.py:52
  87.5 33.1 %collective-permute-start.10 = (f32[8,8,1024]{2,1,0:T(8,128)S(1)}, f32[8,8,1024]{2,1,0:T(8,128)S(1)}, u32[]{:S(2)}, u32[]{:S(2)}) collective-permute-start(f32[8,8,1024]{2,1,0:T(8,128)S(1)} %copy-done.13), channel_id=1, source_target_pairs={{0,1},{1,0},{2,3},{3,2},{4,5},{5,4},{6,7},{7,6},{8,9},{9,8},{10,11... | collective-permute-start | bytes 786440 | tf_op jit(solution)/shard_map/ppermute | solution.py:52
  87.6 33.0 %collective-permute-start.14 = (f32[8,8,1024]{2,1,0:T(8,128)S(1)}, f32[8,8,1024]{2,1,0:T(8,128)S(1)}, u32[]{:S(2)}, u32[]{:S(2)}) collective-permute-start(f32[8,8,1024]{2,1,0:T(8,128)S(1)} %copy-done.10), channel_id=1, source_target_pairs={{0,4},{1,5},{2,6},{3,7},{4,0},{5,1},{6,2},{7,3},{8,12},{9,13},{10,... | collective-permute-start | bytes 786440 | tf_op jit(solution)/shard_map/ppermute | solution.py:52
  95.5 25.2 %collective-permute-start.11 = (f32[8,8,1024]{2,1,0:T(8,128)S(1)}, f32[8,8,1024]{2,1,0:T(8,128)S(1)}, u32[]{:S(2)}, u32[]{:S(2)}) collective-permute-start(f32[8,8,1024]{2,1,0:T(8,128)S(1)} %get-tuple-element.103), channel_id=1, source_target_pairs={{0,2},{1,3},{2,0},{3,1},{4,6},{5,7},{6,4},{7,5},{8,10},{9,11},{10,... | collective-permute-start | bytes 786440 | tf_op jit(solution)/shard_map/ppermute | solution.py:52
  95.5 17.9 %collective-permute-start.22 = (f32[6,8,1024]{2,1,0:T(8,128)}, f32[6,8,1024]{2,1,0:T(8,128)S(1)}, u32[]{:S(2)}, u32[]{:S(2)}) collective-permute-start(f32[6,8,1024]{2,1,0:T(8,128)} %get-tuple-element.123), channel_id=1, source_target_pairs={{0,7},{1,6},{2,5},{3,4},{4,3},{5,2},{6,1},{7,0},{8,15},{9,14},{10,... | collective-permute-start | bytes 589832 | tf_op jit(solution)/shard_map/ppermute | solution.py:52
  113.4 36.8 %collective-permute-start.23 = (f32[6,8,1024]{2,1,0:T(8,128)}, f32[6,8,1024]{2,1,0:T(8,128)S(1)}, u32[]{:S(2)}, u32[]{:S(2)}) collective-permute-start(f32[6,8,1024]{2,1,0:T(8,128)} %get-tuple-element.124), channel_id=1, source_target_pairs={{0,4},{1,5},{2,6},{3,7},{4,0},{5,1},{6,2},{7,3},{8,12},{9,13},{10,... | collective-permute-start | bytes 589832 | tf_op jit(solution)/shard_map/ppermute | solution.py:52
  120.6 34.5 %collective-permute-start.24 = (f32[6,8,1024]{2,1,0:T(8,128)}, f32[6,8,1024]{2,1,0:T(8,128)S(1)}, u32[]{:S(2)}, u32[]{:S(2)}) collective-permute-start(f32[6,8,1024]{2,1,0:T(8,128)} %get-tuple-element.126), channel_id=1, source_target_pairs={{0,5},{1,4},{2,7},{3,6},{4,1},{5,0},{6,3},{7,2},{8,13},{9,12},{10,... | collective-permute-start | bytes 589832 | tf_op jit(solution)/shard_map/ppermute | solution.py:52
  126.3 13.9 %collective-permute-start.16 = (f32[1,4,64,128]{3,2,1,0:T(8,128)S(1)}, f32[1,4,64,128]{3,2,1,0:T(8,128)S(1)}, u32[]{:S(2)}, u32[]{:S(2)}) collective-permute-start(f32[1,4,64,128]{3,2,1,0:T(8,128)S(1)} %get-tuple-element.112), channel_id=1, source_target_pairs={{1,0},{2,1},{3,2},{4,3},{5,4},{6,5},{7,6},{8,7},{9,8},{10,9},{11,1... | collective-permute-start | bytes 393224 | tf_op jit(solution)/shard_map/ppermute | solution.py:52
  127.6 12.6 %collective-permute-start.18 = (f32[1,4,64,128]{3,2,1,0:T(8,128)S(1)}, f32[1,4,64,128]{3,2,1,0:T(8,128)S(1)}, u32[]{:S(2)}, u32[]{:S(2)}) collective-permute-start(f32[1,4,64,128]{3,2,1,0:T(8,128)S(1)} %get-tuple-element.115), channel_id=1, source_target_pairs={{0,1},{1,2},{2,3},{3,4},{4,5},{5,6},{6,7},{7,8},{8,9},{9,10},{10,1... | collective-permute-start | bytes 393224 | tf_op jit(solution)/shard_map/ppermute | solution.py:52
  130.9 27.4 %collective-permute-start.20 = (f32[6,8,1024]{2,1,0:T(8,128)}, f32[6,8,1024]{2,1,0:T(8,128)S(1)}, u32[]{:S(2)}, u32[]{:S(2)}) collective-permute-start(f32[6,8,1024]{2,1,0:T(8,128)} %get-tuple-element.119), channel_id=1, source_target_pairs={{0,6},{1,7},{2,4},{3,5},{4,2},{5,3},{6,0},{7,1},{8,14},{9,15},{10,... | collective-permute-start | bytes 589832 | tf_op jit(solution)/shard_map/ppermute | solution.py:52
  150.1 32.5 %collective-permute-start.25 = (f32[10,8,1024]{2,1,0:T(8,128)}, f32[10,8,1024]{2,1,0:T(8,128)S(1)}, u32[]{:S(2)}, u32[]{:S(2)}) collective-permute-start(f32[10,8,1024]{2,1,0:T(8,128)} %get-tuple-element.131), channel_id=1, source_target_pairs={{0,6},{1,7},{2,4},{3,5},{4,2},{5,3},{6,0},{7,1},{8,14},{9,15},{10,... | collective-permute-start | bytes 983048 | tf_op jit(solution)/shard_map/ppermute | solution.py:52
  155.1 27.9 %collective-permute-start.29 = (f32[10,8,1024]{2,1,0:T(8,128)}, f32[10,8,1024]{2,1,0:T(8,128)S(1)}, u32[]{:S(2)}, u32[]{:S(2)}) collective-permute-start(f32[10,8,1024]{2,1,0:T(8,128)} %get-tuple-element.139), channel_id=1, source_target_pairs={{0,7},{1,6},{2,5},{3,4},{4,3},{5,2},{6,1},{7,0},{8,15},{9,14},{10,... | collective-permute-start | bytes 983048 | tf_op jit(solution)/shard_map/ppermute | solution.py:52
  158.3 16.9 %collective-permute-start.21 = (f32[6,8,1024]{2,1,0:T(8,128)S(1)}, f32[6,8,1024]{2,1,0:T(8,128)S(1)}, u32[]{:S(2)}, u32[]{:S(2)}) collective-permute-start(f32[6,8,1024]{2,1,0:T(8,128)S(1)} %copy-done.30), channel_id=1, source_target_pairs={{0,3},{1,2},{2,1},{3,0},{4,7},{5,6},{6,5},{7,4},{8,11},{9,10},{10,... | collective-permute-start | bytes 589832 | tf_op jit(solution)/shard_map/ppermute | solution.py:52
  158.3 18.5 %collective-permute-start.17 = (f32[6,8,1024]{2,1,0:T(8,128)S(1)}, f32[6,8,1024]{2,1,0:T(8,128)S(1)}, u32[]{:S(2)}, u32[]{:S(2)}) collective-permute-start(f32[6,8,1024]{2,1,0:T(8,128)S(1)} %copy-done.29), channel_id=1, source_target_pairs={{0,1},{1,0},{2,3},{3,2},{4,5},{5,4},{6,7},{7,6},{8,9},{9,8},{10,11... | collective-permute-start | bytes 589832 | tf_op jit(solution)/shard_map/ppermute | solution.py:52
  159.4 20.0 %collective-permute-start.19 = (f32[6,8,1024]{2,1,0:T(8,128)S(1)}, f32[6,8,1024]{2,1,0:T(8,128)S(1)}, u32[]{:S(2)}, u32[]{:S(2)}) collective-permute-start(f32[6,8,1024]{2,1,0:T(8,128)S(1)} %copy-done.28), channel_id=1, source_target_pairs={{0,2},{1,3},{2,0},{3,1},{4,6},{5,7},{6,4},{7,5},{8,10},{9,11},{10,... | collective-permute-start | bytes 589832 | tf_op jit(solution)/shard_map/ppermute | solution.py:52
  175.2 13.3 %collective-permute-start.28 = (f32[10,8,1024]{2,1,0:T(8,128)}, f32[10,8,1024]{2,1,0:T(8,128)S(1)}, u32[]{:S(2)}, u32[]{:S(2)}) collective-permute-start(f32[10,8,1024]{2,1,0:T(8,128)} %get-tuple-element.136), channel_id=1, source_target_pairs={{0,3},{1,2},{2,1},{3,0},{4,7},{5,6},{6,5},{7,4},{8,11},{9,10},{10,... | collective-permute-start | bytes 983048 | tf_op jit(solution)/shard_map/ppermute | solution.py:52
  179.3 19.8 %collective-permute-start.31 = (f32[10,8,1024]{2,1,0:T(8,128)}, f32[10,8,1024]{2,1,0:T(8,128)S(1)}, u32[]{:S(2)}, u32[]{:S(2)}) collective-permute-start(f32[10,8,1024]{2,1,0:T(8,128)} %get-tuple-element.142), channel_id=1, source_target_pairs={{0,5},{1,4},{2,7},{3,6},{4,1},{5,0},{6,3},{7,2},{8,13},{9,12},{10,... | collective-permute-start | bytes 983048 | tf_op jit(solution)/shard_map/ppermute | solution.py:52
  180.2 22.3 %collective-permute-start.27 = (f32[10,8,1024]{2,1,0:T(8,128)}, f32[10,8,1024]{2,1,0:T(8,128)S(1)}, u32[]{:S(2)}, u32[]{:S(2)}) collective-permute-start(f32[10,8,1024]{2,1,0:T(8,128)} %get-tuple-element.134), channel_id=1, source_target_pairs={{0,2},{1,3},{2,0},{3,1},{4,6},{5,7},{6,4},{7,5},{8,10},{9,11},{10,... | collective-permute-start | bytes 983048 | tf_op jit(solution)/shard_map/ppermute | solution.py:52
  182.7 19.8 %collective-permute-start.26 = (f32[10,8,1024]{2,1,0:T(8,128)}, f32[10,8,1024]{2,1,0:T(8,128)S(1)}, u32[]{:S(2)}, u32[]{:S(2)}) collective-permute-start(f32[10,8,1024]{2,1,0:T(8,128)} %get-tuple-element.132), channel_id=1, source_target_pairs={{0,1},{1,0},{2,3},{3,2},{4,5},{5,4},{6,7},{7,6},{8,9},{9,8},{10,11... | collective-permute-start | bytes 983048 | tf_op jit(solution)/shard_map/ppermute | solution.py:52
  183.0 30.0 %collective-permute-start.30 = (f32[10,8,1024]{2,1,0:T(8,128)}, f32[10,8,1024]{2,1,0:T(8,128)S(1)}, u32[]{:S(2)}, u32[]{:S(2)}) collective-permute-start(f32[10,8,1024]{2,1,0:T(8,128)} %get-tuple-element.140), channel_id=1, source_target_pairs={{0,4},{1,5},{2,6},{3,7},{4,0},{5,1},{6,2},{7,3},{8,12},{9,13},{10,... | collective-permute-start | bytes 983048 | tf_op jit(solution)/shard_map/ppermute | solution.py:52
  (31 other events, 559.7 us)

commit v3 on v2

--- a/solution.py
+++ b/solution.py
@@ -12,7 +12,7 @@
 R = 8
 LANES = 128
 BATCH = 16
-SECTIONS = 2
+SECTIONS = 4
 FLIGHT = 5
 SECTION_MIB = 58
 BORDER_MIB = 32
@@ -100,8 +100,9 @@
     size = plan.size
     early = [refs.pop(0) for _ in range(size)] if plan.early else []
     kept = refs.pop(0)
-    halos = [refs.pop(0) for _ in range(2)] if section else []
-    edges = [refs.pop(0) for _ in range(4)] if section else []
+    first_one = section == plan.sections - 1
+    halos = [refs.pop(0) for _ in range(2)] if first_one else []
+    edges = [refs.pop(0) for _ in range(4)] if first_one else []
     q_win, n_win, buf_a, buf_b, coef, sems = refs
     members, window, lon = q_win.shape
     height = size * plan.tile
@@ -111,7 +112,7 @@
         pltpu.make_async_copy(numbers.at[:, pl.ds(start, window), :], n_win, sems.at[0]),
         pltpu.make_async_copy(q.at[:, pl.ds(start, window), :], q_win, sems.at[1]),
     ]
-    for i, first in enumerate((0, plan.rows - 8)) if section else []:
+    for i, first in enumerate((0, plan.rows - 8)) if first_one else []:
         rows = pl.ds(first, 8)
         copies.append(pltpu.make_async_copy(q.at[:, rows, :], edges[2 * i], sems.at[2 + 2 * i]))
         copies.append(
@@ -150,7 +151,7 @@
             kept[i, slot] = src[first + row]
     for copy in copies[2:]:
         copy.wait()
-    for side in range(2) if section else []:
+    for side in range(2) if first_one else []:
         first = 0 if side == 0 else 8 - STEPS
         fields, stencil = edges[2 * side : 2 * side + 2]
         turned = jnp.swapaxes(fields[...], 0, 1)
@@ -391,7 +392,7 @@
             shapes = [sds(early_rows, share, lon)] * size
         shapes.append(sds(size, late_rows, share, lon))
         scratch = []
-        if section:
+        if section == plan.sections - 1:
             shapes += [sds(STEPS, share + 8, lon)] * 2
             scratch = [pltpu.VMEM((share, 8, lon), f32), pltpu.VMEM((3, 8, lon), f32)] * 2
         return pl.pallas_call(
@@ -413,18 +414,22 @@
             name=f"section_{section}",
         )(order, initial, stencil_numbers)
 
-    far_outs = forecast(1, place)
-    near_outs = forecast(0, after(place, far_outs[-1]))
-    kept_far, kept_near = far_outs[-3], near_outs[-1]
+    order, early, kept = place, [], []
+    for section in reversed(range(plan.sections)):
+        outs = list(forecast(section, order))
+        if section == plan.sections - 1:
+            to_high, to_low = outs.pop(), outs.pop()
+        kept.insert(0, outs.pop())
+        early = outs + early
+        order = after(place, kept[0])
     if plan.early:
-        early = near_outs[:size] + far_outs[:size]
-        low = chain.shift(far_outs[-1], "slab", 1)
         early = send(early, far[:2])
-        high = chain.shift(far_outs[-2], "slab", -1)
+        low = chain.shift(to_high, "slab", 1)
+        high = chain.shift(to_low, "slab", -1)
         early = send(early, far[2:3] + [r for r in turns[2:] if r != far[2]])
     else:
-        low = chain.shift(far_outs[-1], "slab", 1)
-        high = chain.shift(far_outs[-2], "slab", -1)
+        low = chain.shift(to_high, "slab", 1)
+        high = chain.shift(to_low, "slab", -1)
     late = pl.pallas_call(
         functools.partial(border_kernel, plan),
         out_shape=[sds(late_rows, share, lon)] * count,
@@ -442,7 +447,7 @@
         compiler_params=params(BORDER_MIB),
         cost_estimate=hint(4),
         name="border",
-    )(place, low, high, initial, stencil_numbers, kept_near, kept_far)
+    )(place, low, high, initial, stencil_numbers, *kept)
 
     blocks = tile * per_row
     first_block = lax.axis_index(("slab", "member")) * blocks
@@ -501,6 +506,9 @@
         fields = made.pop(0) if keep_fields else None
         return mixing, fields, made
 
+    order_b = near[:-1] + far + near[-1:]
+    order_c = far + near
+    order_d = turns
     slots = lambda rows: [(row, slot) for slot, row in enumerate(rows)]
     parts, returned = [], []
     inner = [r for r in plan.early if r - 1 in plan.early and r + 1 in plan.early]
@@ -512,13 +520,13 @@
         )
         old_mix = [(slots(plan.early), mixing)]
         old_fields = [(slots(edge), fields)] if edge else []
-        late = send(late, turns, fields if edge else mixing)
+        late = send(late, order_b, fields if edge else mixing)
         order = after(place, mixing)
         if inner:
             parts.append(inner)
-            back = send(back, far[:2])
+            back = send(back, order_c[:1])
     else:
-        late = send(late, turns)
+        late = send(late, order_b)
     rims = sorted({0, tile - 1})
     rest = [r for r in plan.late if r not in rims]
     mixing, _, _ = analyse(plan.late, late, rims, [], [], [], [], "mix_rims", order)
@@ -526,7 +534,9 @@
     from_prev = chain.shift(mixing[rims.index(tile - 1)][None], axes, 1)
     from_next = chain.shift(mixing[0][None], axes, -1)
     if inner:
-        returned += send(back, far[2:] + near)
+        for r in order_c[1:]:
+            back[r] = after(back[r], mixing)
+        returned += send(back, order_c[1:])
     old_mix += [(slots(rims), mixing), ([(-1, 0)], from_prev), ([(tile, 0)], from_next)]
     if rest:
         mixing, _, _ = analyse(plan.late, late, rest, [], [], [], [], "mix_late", after(place, mixing))
@@ -534,7 +544,7 @@
     others = [r for r in range(tile) if r not in inner]
     _, _, back = analyse(plan.late, late, [], old_mix, old_fields, others, [], "analyse_late")
     parts.append(others)
-    returned += send(back, turns)
+    returned += send(back, order_d)
 
     return pl.pallas_call(
         functools.partial(assemble_kernel, plan, parts),

time: 218 us -> 210 us (0.963)
  starting transfers between devices: 76 us -> 57.1 us
  Pallas kernels: 56.7 us -> 63.4 us
  waiting for transfers between devices: 69.4 us -> 73.2 us
    ppermute x32, starting transfers between devices: 76 us -> 57.1 us  [permute(): self.ended.append(lax.ppermute(piece, axis, route))]
    pallas_call x2 -> x4, Pallas kernels: 21.9 us -> 28.1 us  [forecast(): pl.pallas_call(functools.partial(section_kernel, plan, section), out_shap...]
    ppermute x32, waiting for transfers between devices: 69.4 us -> 73.2 us  [permute(): self.ended.append(lax.ppermute(piece, axis, route))]
    unnamed x63 -> x65, local copies, waits for them, and re-layouts: 11 us -> 11.5 us
  transfers between devices with their start and end apart: 32 -> 32, of which waited for: 8 -> 8; matrix products, arithmetic and copies ran while one was open for 2% -> 2% of each run, Pallas kernels for 19% -> 25%
where the time goes in v3:
time: 210 us
  waiting for transfers between devices  73.2 us (35%)
  Pallas kernels  63.4 us (30%)
  starting transfers between devices  57.1 us (27%)
  local copies, waits for them, and re-layouts  15.2 us (7%)
    ppermute x32, waiting for transfers between devices, permute(): self.ended.append(lax.ppermute(piece, axis, route))  73.2 us
    ppermute x32, starting transfers between devices, permute(): self.ended.append(lax.ppermute(piece, axis, route))  57.1 us
    pallas_call x4, Pallas kernels, analyse(): pl.pallas_call(functools.partial(analysis_kernel, plan, arrived, fresh, [...  28.1 us
    pallas_call x4, Pallas kernels, forecast(): pl.pallas_call(functools.partial(section_kernel, plan, section), out_shap...  28.1 us
    unnamed x65, local copies, waits for them, and re-layouts  11.5 us
  transfers between devices with their start and end apart: 32, of which 8 were waited for; matrix products, arithmetic and copies ran while one was open for 2% of the time, Pallas kernels for 25%

profile of v3, /device:TPU:0, one launch (start us, length us, event | category | flops | bytes accessed | tf_op | source)
XLA Modules:
  0.0 209.8 jit_solution(7668805321697188045)
XLA Ops:
  0.6 7.2 %section_3.1 = (f32[8,8,1024]{2,1,0:T(8,128)}, f32[8,8,1024]{2,1,0:T(8,128)}, f32[2,8,8,1024]{3,2,1,0:T(8,128)}, f32[4,16,1024]{2,1,0:T(8,128)}, f32[4,16,1024]{2,1,0:T(8,128)}) custom-call(s32[5]{0:T(128)} %stack.23.place.refs_0_, f32[8,128,1024]{2,1,0:T(8,128)} %q.9, f32[3,128,1024]{2,1,0:T(8,128)} %numbers.9), custom_call_target="tpu_custom_call" | custom-call | bytes 33210000 | tf_op jit(solution)/shard_map/section_3/pallas_call | solution.py:398
  7.8 4.6 %collective-permute-start.4 = (f32[8,8,1024]{2,1,0:T(8,128)}, f32[8,8,1024]{2,1,0:T(8,128)}, u32[]{:S(2)}, u32[]{:S(2)}) collective-permute-start(f32[8,8,1024]{2,1,0:T(8,128)} %get-tuple-element.98), channel_id=1, source_target_pairs={{0,7},{1,6},{2,5},{3,4},{4,3},{5,2},{6,1},{7,0},{8,15},{9,14},{10,... | collective-permute-start | bytes 786440 | tf_op jit(solution)/shard_map/ppermute | solution.py:52
  14.3 5.3 %collective-permute-start.6 = (f32[4,16,1024]{2,1,0:T(8,128)}, f32[4,16,1024]{2,1,0:T(8,128)}, u32[]{:S(2)}, u32[]{:S(2)}) collective-permute-start(f32[4,16,1024]{2,1,0:T(8,128)} %get-tuple-element.101), channel_id=1, source_target_pairs={{0,8},{8,16},{16,24},{1,9},{9,17},{17,25},{2,10},{10,18},{18,26},{... | collective-permute-start | bytes 786440 | tf_op jit(solution)/shard_map/ppermute | solution.py:52
  19.6 7.0 %section_2.1 = (f32[8,8,1024]{2,1,0:T(8,128)}, f32[8,8,1024]{2,1,0:T(8,128)}, f32[2,8,8,1024]{3,2,1,0:T(8,128)}) custom-call(s32[5]{0:T(128)} %stack.23.place.refs_0_, f32[8,128,1024]{2,1,0:T(8,128)} %q.9, f32[3,128,1024]{2,1,0:T(8,128)} %numbers.9), custom_call_target="tpu_custom_call" | custom-call | bytes 33210000 | tf_op jit(solution)/shard_map/section_2/pallas_call | solution.py:398
  26.7 7.0 %section_1.1 = (f32[8,8,1024]{2,1,0:T(8,128)}, f32[8,8,1024]{2,1,0:T(8,128)}, f32[2,8,8,1024]{3,2,1,0:T(8,128)}) custom-call(s32[5]{0:T(128)} %stack.23.place.refs_0_, f32[8,128,1024]{2,1,0:T(8,128)} %q.9, f32[3,128,1024]{2,1,0:T(8,128)} %numbers.9), custom_call_target="tpu_custom_call" | custom-call | bytes 33210000 | tf_op jit(solution)/shard_map/section_1/pallas_call | solution.py:398
  33.7 3.5 %collective-permute-start.5 = (f32[8,8,1024]{2,1,0:T(8,128)}, f32[8,8,1024]{2,1,0:T(8,128)}, u32[]{:S(2)}, u32[]{:S(2)}) collective-permute-start(f32[8,8,1024]{2,1,0:T(8,128)} %get-tuple-element.99), channel_id=1, source_target_pairs={{0,3},{1,2},{2,1},{3,0},{4,7},{5,6},{6,5},{7,4},{8,11},{9,10},{10,... | collective-permute-start | bytes 786440 | tf_op jit(solution)/shard_map/ppermute | solution.py:52
  37.2 7.0 %section_0.1 = (f32[8,8,1024]{2,1,0:T(8,128)}, f32[8,8,1024]{2,1,0:T(8,128)}, f32[2,8,8,1024]{3,2,1,0:T(8,128)}) custom-call(s32[5]{0:T(128)} %stack.23.place.refs_0_, f32[8,128,1024]{2,1,0:T(8,128)} %q.9, f32[3,128,1024]{2,1,0:T(8,128)} %numbers.9), custom_call_target="tpu_custom_call" | custom-call | bytes 33210000 | tf_op jit(solution)/shard_map/section_0/pallas_call | solution.py:398
  44.6 1.9 collective-permute-start.7
  50.7 3.4 %border.1 = (f32[8,8,1024]{2,1,0:T(8,128)S(1)}, f32[8,8,1024]{2,1,0:T(8,128)S(1)}, f32[8,8,1024]{2,1,0:T(8,128)}, f32[8,8,1024]{2,1,0:T(8,128)}, f32[8,8,1024]{2...) custom-call(s32[5]{0:T(128)S(1)} %copy-done.9, ...), custom_call_target="tpu_custom_call" | custom-call | bytes 14760000 | tf_op jit(solution)/shard_map/border/pallas_call | solution.py:433
  58.8 1.7 collective-permute-start.9
  64.3 1.9 collective-permute-start.14
  68.0 1.5 collective-permute-start.13
  69.5 10.0 %analyse_early.1 = (f32[8,4,64,128]{3,2,1,0:T(8,128)}, f32[2,64,1024]{2,1,0:T(8,128)}, f32[6,8,1024]{2,1,0:T(8,128)}, f32[6,8,1024]{2,1,0:T(8,128)}, f32[6,8,102...) custom-call(s32[5]{0:T(128)} %stack.23.place.refs_0_, ...), custom_call_target="tpu_custom_call" | custom-call | bytes 35424000 | tf_op jit(solution)/shard_map/analyse_early/pallas_call | solution.py:482
  80.3 1.8 collective-permute-start.22
  82.6 2.3 %collective-permute-done.14.refs_9_ = f32[8,8,1024]{2,1,0:T(8,128)S(1)} collective-permute-done((f32[8,8,1024]{2,1,0:T(8,128)}, f32[8,8,1024]{2,1,0:T(8,128)S(1)}, u32[]{:S(2)}, u32[]{:S(2)}) %collective-permute-start.14) | collective-permute-done | bytes 262176 | tf_op jit(solution)/shard_map/ppermute | solution.py:52
  84.9 23.0 %collective-permute-done.12.refs_7_ = f32[8,8,1024]{2,1,0:T(8,128)S(1)} collective-permute-done((f32[8,8,1024]{2,1,0:T(8,128)}, f32[8,8,1024]{2,1,0:T(8,128)S(1)}, u32[]{:S(2)}, u32[]{:S(2)}) %collective-permute-start.12) | collective-permute-done | bytes 262176 | tf_op jit(solution)/shard_map/ppermute | solution.py:52
  107.9 5.5 %collective-permute-done.13.refs_8_ = f32[8,8,1024]{2,1,0:T(8,128)S(1)} collective-permute-done((f32[8,8,1024]{2,1,0:T(8,128)}, f32[8,8,1024]{2,1,0:T(8,128)S(1)}, u32[]{:S(2)}, u32[]{:S(2)}) %collective-permute-start.13) | collective-permute-done | bytes 262176 | tf_op jit(solution)/shard_map/ppermute | solution.py:52
  114.1 3.7 %mix_rims.1.refs_13_ = f32[2,4,64,128]{3,2,1,0:T(8,128)} custom-call(s32[5]{0:T(128)} %stack.23.place.refs_0_, s32[2]{0:T(128)} %iota_multiply_fusion.refs_1_, s32[1]{0:T(128)} %constant.77.clone.refs_2_.refs_1_, f32[8,8,1024]{2,1,0:T(8,128)} %copy-done.2, f32[8,8,1024]{2,1,0:T(8,128)} %copy-done.23, f32[8,8,1024]{2,1,0:T(8,128)} %copy-done.18, ...), custom_call_target="tpu_custom_call" | custom-call | tf_op jit(solution)/shard_map/mix_rims/pallas_call | solution.py:482
  122.5 3.4 %collective-permute-start.20 = (f32[1,4,64,128]{3,2,1,0:T(8,128)S(1)}, f32[1,4,64,128]{3,2,1,0:T(8,128)S(1)}, u32[]{:S(2)}, u32[]{:S(2)}) collective-permute-start(f32[1,4,64,128]{3,2,1,0:T(8,128)S(1)} %get-tuple-element.137), channel_id=1, source_target_pairs={{0,1},{1,2},{2,3},{3,4},{4,5},{5,6},{6,7},{7,8},{8,9},{9,10},{10,1... | collective-permute-start | bytes 393224 | tf_op jit(solution)/shard_map/ppermute | solution.py:52
  126.0 2.4 %collective-permute-start.16 = (f32[6,8,1024]{2,1,0:T(8,128)}, f32[6,8,1024]{2,1,0:T(8,128)S(1)}, u32[]{:S(2)}, u32[]{:S(2)}) collective-permute-start(f32[6,8,1024]{2,1,0:T(8,128)} %get-tuple-element.129), channel_id=1, source_target_pairs={{0,6},{1,7},{2,4},{3,5},{4,2},{5,3},{6,0},{7,1},{8,14},{9,15},{10,... | collective-permute-start | bytes 589832 | tf_op jit(solution)/shard_map/ppermute | solution.py:52
  128.4 5.8 %mix_late.1.refs_16_ = f32[6,4,64,128]{3,2,1,0:T(8,128)} custom-call(s32[5]{0:T(128)} %stack.23.place.refs_0_, s32[6]{0:T(128)} %constant.78.clone.refs_1_, s32[1]{0:T(128)} %constant.77.clone.refs_2_.refs_1_, f32[8,8,1024]{2,1,0:T(8,128)} %copy-done.2, f32[8,8,1024]{2,1,0:T(8,128)} %copy-done.23, f32[8,8,1024]{2,1,0:T(8,128)} %copy-done.18, ...), custom_call_target="tpu_custom_call" | custom-call | tf_op jit(solution)/shard_map/mix_late/pallas_call | solution.py:482
  135.4 8.6 %analyse_late.1 = (f32[10,8,1024]{2,1,0:T(8,128)}, f32[10,8,1024]{2,1,0:T(8,128)}, f32[10,8,1024]{2,1,0:T(8,128)}, f32[10,8,1024]{2,1,0:T(8,128)}, f32[10,8,1024...) custom-call(s32[5]{0:T(128)} %stack.23.place.refs_0_, ...), custom_call_target="tpu_custom_call" | custom-call | tf_op jit(solution)/shard_map/analyse_late/pallas_call | solution.py:482
  144.0 4.3 %collective-permute-start.29 = (f32[10,8,1024]{2,1,0:T(8,128)}, f32[10,8,1024]{2,1,0:T(8,128)S(1)}, u32[]{:S(2)}, u32[]{:S(2)}) collective-permute-start(f32[10,8,1024]{2,1,0:T(8,128)} %get-tuple-element.159), channel_id=1, source_target_pairs={{0,7},{1,6},{2,5},{3,4},{4,3},{5,2},{6,1},{7,0},{8,15},{9,14},{10,... | collective-permute-start | bytes 983048 | tf_op jit(solution)/shard_map/ppermute | solution.py:52
  148.3 3.4 %collective-permute-start.25 = (f32[10,8,1024]{2,1,0:T(8,128)}, f32[10,8,1024]{2,1,0:T(8,128)S(1)}, u32[]{:S(2)}, u32[]{:S(2)}) collective-permute-start(f32[10,8,1024]{2,1,0:T(8,128)} %get-tuple-element.151), channel_id=1, source_target_pairs={{0,6},{1,7},{2,4},{3,5},{4,2},{5,3},{6,0},{7,1},{8,14},{9,15},{10,... | collective-permute-start | bytes 983048 | tf_op jit(solution)/shard_map/ppermute | solution.py:52
  151.7 5.2 %collective-permute-start.21 = (f32[6,8,1024]{2,1,0:T(8,128)S(1)}, f32[6,8,1024]{2,1,0:T(8,128)S(1)}, u32[]{:S(2)}, u32[]{:S(2)}) collective-permute-start(f32[6,8,1024]{2,1,0:T(8,128)S(1)} %copy-done.31), channel_id=1, source_target_pairs={{0,3},{1,2},{2,1},{3,0},{4,7},{5,6},{6,5},{7,4},{8,11},{9,10},{10,... | collective-permute-start | bytes 589832 | tf_op jit(solution)/shard_map/ppermute | solution.py:52
  156.9 1.9 collective-permute-start.19
  158.9 9.1 %collective-permute-done.21.refs_3_ = f32[6,8,1024]{2,1,0:T(8,128)S(1)} collective-permute-done((f32[6,8,1024]{2,1,0:T(8,128)S(1)}, f32[6,8,1024]{2,1,0:T(8,128)S(1)}, u32[]{:S(2)}, u32[]{:S(2)}) %collective-permute-start.21) | collective-permute-done | bytes 196640 | tf_op jit(solution)/shard_map/ppermute | solution.py:52
  168.0 4.3 %collective-permute-done.19.refs_2_ = f32[6,8,1024]{2,1,0:T(8,128)S(1)} collective-permute-done((f32[6,8,1024]{2,1,0:T(8,128)S(1)}, f32[6,8,1024]{2,1,0:T(8,128)S(1)}, u32[]{:S(2)}, u32[]{:S(2)}) %collective-permute-start.19) | collective-permute-done | bytes 196640 | tf_op jit(solution)/shard_map/ppermute | solution.py:52
  173.5 2.5 %collective-permute-start.28 = (f32[10,8,1024]{2,1,0:T(8,128)}, f32[10,8,1024]{2,1,0:T(8,128)S(1)}, u32[]{:S(2)}, u32[]{:S(2)}) collective-permute-start(f32[10,8,1024]{2,1,0:T(8,128)} %get-tuple-element.156), channel_id=1, source_target_pairs={{0,3},{1,2},{2,1},{3,0},{4,7},{5,6},{6,5},{7,4},{8,11},{9,10},{10,... | collective-permute-start | bytes 983048 | tf_op jit(solution)/shard_map/ppermute | solution.py:52
  177.0 13.6 %collective-permute-done.31.refs_13_ = f32[10,8,1024]{2,1,0:T(8,128)S(1)} collective-permute-done((f32[10,8,1024]{2,1,0:T(8,128)}, f32[10,8,1024]{2,1,0:T(8,128)S(1)}, u32[]{:S(2)}, u32[]{:S(2)}) %collective-permute-start.31) | collective-permute-done | bytes 327712 | tf_op jit(solution)/shard_map/ppermute | solution.py:52
  190.7 14.4 %collective-permute-done.27.refs_10_ = f32[10,8,1024]{2,1,0:T(8,128)S(1)} collective-permute-done((f32[10,8,1024]{2,1,0:T(8,128)}, f32[10,8,1024]{2,1,0:T(8,128)S(1)}, u32[]{:S(2)}, u32[]{:S(2)}) %collective-permute-start.27) | collective-permute-done | bytes 327712 | tf_op jit(solution)/shard_map/ppermute | solution.py:52
  206.1 3.7 %assemble.1 = f32[8,128,1024]{2,1,0:T(8,128)} custom-call(s32[5]{0:T(128)S(1)} %copy-done.10, f32[6,8,1024]{2,1,0:T(8,128)S(1)} %copy-done.8, f32[6,8,1024]{2,1,0:T(8,128)S(1)} %collective-permute-done.17.refs_1_, f32[6,8,1024]{2,1,0:T(8,128)S(1)} %collective-permute-done.19.refs_2_, f32[6,8,1024]{2,1,0:T(8,128)S(1)} %collective-permute-done.21.refs_3_, ...), custom_call_target="tpu_custom_call" | custom-call | bytes 14760000 | tf_op jit(solution)/shard_map/assemble/pallas_call | solution.py:549
  (117 shorter events, 28.6 us)
Async XLA Ops:
  7.8 25.9 %collective-permute-start.4 = (f32[8,8,1024]{2,1,0:T(8,128)}, f32[8,8,1024]{2,1,0:T(8,128)}, u32[]{:S(2)}, u32[]{:S(2)}) collective-permute-start(f32[8,8,1024]{2,1,0:T(8,128)} %get-tuple-element.98), channel_id=1, source_target_pairs={{0,7},{1,6},{2,5},{3,4},{4,3},{5,2},{6,1},{7,0},{8,15},{9,14},{10,... | collective-permute-start | bytes 786440 | tf_op jit(solution)/shard_map/ppermute | solution.py:52
  12.4 31.8 %collective-permute-start.2 = (f32[8,8,1024]{2,1,0:T(8,128)}, f32[8,8,1024]{2,1,0:T(8,128)}, u32[]{:S(2)}, u32[]{:S(2)}) collective-permute-start(f32[8,8,1024]{2,1,0:T(8,128)} %get-tuple-element.95), channel_id=1, source_target_pairs={{0,6},{1,7},{2,4},{3,5},{4,2},{5,3},{6,0},{7,1},{8,14},{9,15},{10,... | collective-permute-start | bytes 786440 | tf_op jit(solution)/shard_map/ppermute | solution.py:52
  13.0 33.5 %collective-permute-start = (f32[4,16,1024]{2,1,0:T(8,128)}, f32[4,16,1024]{2,1,0:T(8,128)S(1)}, u32[]{:S(2)}, u32[]{:S(2)}) collective-permute-start(f32[4,16,1024]{2,1,0:T(8,128)} %get-tuple-element.92), channel_id=1, source_target_pairs={{8,0},{16,8},{24,16},{9,1},{17,9},{25,17},{10,2},{18,10},{26,18},{... | collective-permute-start | bytes 786440 | tf_op jit(solution)/shard_map/ppermute | solution.py:52
  14.3 30.3 %collective-permute-start.6 = (f32[4,16,1024]{2,1,0:T(8,128)}, f32[4,16,1024]{2,1,0:T(8,128)}, u32[]{:S(2)}, u32[]{:S(2)}) collective-permute-start(f32[4,16,1024]{2,1,0:T(8,128)} %get-tuple-element.101), channel_id=1, source_target_pairs={{0,8},{8,16},{16,24},{1,9},{9,17},{17,25},{2,10},{10,18},{18,26},{... | collective-permute-start | bytes 786440 | tf_op jit(solution)/shard_map/ppermute | solution.py:52
  26.6 31.8 %collective-permute-start.8 = (f32[8,8,1024]{2,1,0:T(8,128)}, f32[8,8,1024]{2,1,0:T(8,128)}, u32[]{:S(2)}, u32[]{:S(2)}) collective-permute-start(f32[8,8,1024]{2,1,0:T(8,128)} %get-tuple-element.103), channel_id=1, source_target_pairs={{0,5},{1,4},{2,7},{3,6},{4,1},{5,0},{6,3},{7,2},{8,13},{9,12},{10,... | collective-permute-start | bytes 786440 | tf_op jit(solution)/shard_map/ppermute | solution.py:52
  33.7 25.1 %collective-permute-start.5 = (f32[8,8,1024]{2,1,0:T(8,128)}, f32[8,8,1024]{2,1,0:T(8,128)}, u32[]{:S(2)}, u32[]{:S(2)}) collective-permute-start(f32[8,8,1024]{2,1,0:T(8,128)} %get-tuple-element.99), channel_id=1, source_target_pairs={{0,3},{1,2},{2,1},{3,0},{4,7},{5,6},{6,5},{7,4},{8,11},{9,10},{10,... | collective-permute-start | bytes 786440 | tf_op jit(solution)/shard_map/ppermute | solution.py:52
  44.2 17.1 %collective-permute-start.3 = (f32[8,8,1024]{2,1,0:T(8,128)}, f32[8,8,1024]{2,1,0:T(8,128)}, u32[]{:S(2)}, u32[]{:S(2)}) collective-permute-start(f32[8,8,1024]{2,1,0:T(8,128)} %get-tuple-element.96), channel_id=1, source_target_pairs={{0,2},{1,3},{2,0},{3,1},{4,6},{5,7},{6,4},{7,5},{8,10},{9,11},{10,... | collective-permute-start | bytes 786440 | tf_op jit(solution)/shard_map/ppermute | solution.py:52
  44.6 19.6 %collective-permute-start.7 = (f32[8,8,1024]{2,1,0:T(8,128)}, f32[8,8,1024]{2,1,0:T(8,128)}, u32[]{:S(2)}, u32[]{:S(2)}) collective-permute-start(f32[8,8,1024]{2,1,0:T(8,128)} %get-tuple-element.102), channel_id=1, source_target_pairs={{0,4},{1,5},{2,6},{3,7},{4,0},{5,1},{6,2},{7,3},{8,12},{9,13},{10,... | collective-permute-start | bytes 786440 | tf_op jit(solution)/shard_map/ppermute | solution.py:52
  58.4 8.8 %collective-permute-start.11 = (f32[8,8,1024]{2,1,0:T(8,128)}, f32[8,8,1024]{2,1,0:T(8,128)S(1)}, u32[]{:S(2)}, u32[]{:S(2)}) collective-permute-start(f32[8,8,1024]{2,1,0:T(8,128)} %get-tuple-element.117), channel_id=1, source_target_pairs={{0,3},{1,2},{2,1},{3,0},{4,7},{5,6},{6,5},{7,4},{8,11},{9,10},{10,... | collective-permute-start | bytes 786440 | tf_op jit(solution)/shard_map/ppermute | solution.py:52
  58.4 9.6 %collective-permute-start.1 = (f32[8,8,1024]{2,1,0:T(8,128)}, f32[8,8,1024]{2,1,0:T(8,128)S(1)}, u32[]{:S(2)}, u32[]{:S(2)}) collective-permute-start(f32[8,8,1024]{2,1,0:T(8,128)} %get-tuple-element.93), channel_id=1, source_target_pairs={{0,1},{1,0},{2,3},{3,2},{4,5},{5,4},{6,7},{7,6},{8,9},{9,8},{10,11... | collective-permute-start | bytes 786440 | tf_op jit(solution)/shard_map/ppermute | solution.py:52
  58.8 20.8 %collective-permute-start.9 = (f32[8,8,1024]{2,1,0:T(8,128)}, f32[8,8,1024]{2,1,0:T(8,128)S(1)}, u32[]{:S(2)}, u32[]{:S(2)}) collective-permute-start(f32[8,8,1024]{2,1,0:T(8,128)} %get-tuple-element.114), channel_id=1, source_target_pairs={{0,2},{1,3},{2,0},{3,1},{4,6},{5,7},{6,4},{7,5},{8,10},{9,11},{10,... | collective-permute-start | bytes 786440 | tf_op jit(solution)/shard_map/ppermute | solution.py:52
  61.3 19.0 %collective-permute-start.15 = (f32[8,8,1024]{2,1,0:T(8,128)}, f32[8,8,1024]{2,1,0:T(8,128)S(1)}, u32[]{:S(2)}, u32[]{:S(2)}) collective-permute-start(f32[8,8,1024]{2,1,0:T(8,128)} %copy-done.16), channel_id=1, source_target_pairs={{0,7},{1,6},{2,5},{3,4},{4,3},{5,2},{6,1},{7,0},{8,15},{9,14},{10,... | collective-permute-start | bytes 786440 | tf_op jit(solution)/shard_map/ppermute | solution.py:52
  64.3 20.6 %collective-permute-start.14 = (f32[8,8,1024]{2,1,0:T(8,128)}, f32[8,8,1024]{2,1,0:T(8,128)S(1)}, u32[]{:S(2)}, u32[]{:S(2)}) collective-permute-start(f32[8,8,1024]{2,1,0:T(8,128)} %copy-done.15), channel_id=1, source_target_pairs={{0,6},{1,7},{2,4},{3,5},{4,2},{5,3},{6,0},{7,1},{8,14},{9,15},{10,... | collective-permute-start | bytes 786440 | tf_op jit(solution)/shard_map/ppermute | solution.py:52
  67.1 40.7 %collective-permute-start.12 = (f32[8,8,1024]{2,1,0:T(8,128)}, f32[8,8,1024]{2,1,0:T(8,128)S(1)}, u32[]{:S(2)}, u32[]{:S(2)}) collective-permute-start(f32[8,8,1024]{2,1,0:T(8,128)} %copy-done.14), channel_id=1, source_target_pairs={{0,4},{1,5},{2,6},{3,7},{4,0},{5,1},{6,2},{7,3},{8,12},{9,13},{10,... | collective-permute-start | bytes 786440 | tf_op jit(solution)/shard_map/ppermute | solution.py:52
  68.0 45.3 %collective-permute-start.13 = (f32[8,8,1024]{2,1,0:T(8,128)}, f32[8,8,1024]{2,1,0:T(8,128)S(1)}, u32[]{:S(2)}, u32[]{:S(2)}) collective-permute-start(f32[8,8,1024]{2,1,0:T(8,128)} %copy-done.13), channel_id=1, source_target_pairs={{0,5},{1,4},{2,7},{3,6},{4,1},{5,0},{6,3},{7,2},{8,13},{9,12},{10,... | collective-permute-start | bytes 786440 | tf_op jit(solution)/shard_map/ppermute | solution.py:52
  79.6 33.8 %collective-permute-start.10 = (f32[8,8,1024]{2,1,0:T(8,128)S(1)}, f32[8,8,1024]{2,1,0:T(8,128)S(1)}, u32[]{:S(2)}, u32[]{:S(2)}) collective-permute-start(f32[8,8,1024]{2,1,0:T(8,128)S(1)} %copy-done.12), channel_id=1, source_target_pairs={{0,1},{1,0},{2,3},{3,2},{4,5},{5,4},{6,7},{7,6},{8,9},{9,8},{10,11... | collective-permute-start | bytes 786440 | tf_op jit(solution)/shard_map/ppermute | solution.py:52
  80.3 37.6 %collective-permute-start.22 = (f32[6,8,1024]{2,1,0:T(8,128)}, f32[6,8,1024]{2,1,0:T(8,128)S(1)}, u32[]{:S(2)}, u32[]{:S(2)}) collective-permute-start(f32[6,8,1024]{2,1,0:T(8,128)} %get-tuple-element.142), channel_id=1, source_target_pairs={{0,7},{1,6},{2,5},{3,4},{4,3},{5,2},{6,1},{7,0},{8,15},{9,14},{10,... | collective-permute-start | bytes 589832 | tf_op jit(solution)/shard_map/ppermute | solution.py:52
  117.9 30.5 %collective-permute-start.23 = (f32[6,8,1024]{2,1,0:T(8,128)}, f32[6,8,1024]{2,1,0:T(8,128)S(1)}, u32[]{:S(2)}, u32[]{:S(2)}) collective-permute-start(f32[6,8,1024]{2,1,0:T(8,128)} %get-tuple-element.143), channel_id=1, source_target_pairs={{0,4},{1,5},{2,6},{3,7},{4,0},{5,1},{6,2},{7,3},{8,12},{9,13},{10,... | collective-permute-start | bytes 589832 | tf_op jit(solution)/shard_map/ppermute | solution.py:52
  118.9 25.1 %collective-permute-start.24 = (f32[6,8,1024]{2,1,0:T(8,128)}, f32[6,8,1024]{2,1,0:T(8,128)S(1)}, u32[]{:S(2)}, u32[]{:S(2)}) collective-permute-start(f32[6,8,1024]{2,1,0:T(8,128)} %get-tuple-element.146), channel_id=1, source_target_pairs={{0,5},{1,4},{2,7},{3,6},{4,1},{5,0},{6,3},{7,2},{8,13},{9,12},{10,... | collective-permute-start | bytes 589832 | tf_op jit(solution)/shard_map/ppermute | solution.py:52
  121.2 12.9 %collective-permute-start.18 = (f32[1,4,64,128]{3,2,1,0:T(8,128)S(1)}, f32[1,4,64,128]{3,2,1,0:T(8,128)S(1)}, u32[]{:S(2)}, u32[]{:S(2)}) collective-permute-start(f32[1,4,64,128]{3,2,1,0:T(8,128)S(1)} %get-tuple-element.133), channel_id=1, source_target_pairs={{1,0},{2,1},{3,2},{4,3},{5,4},{6,5},{7,6},{8,7},{9,8},{10,9},{11,1... | collective-permute-start | bytes 393224 | tf_op jit(solution)/shard_map/ppermute | solution.py:52
  122.5 11.6 %collective-permute-start.20 = (f32[1,4,64,128]{3,2,1,0:T(8,128)S(1)}, f32[1,4,64,128]{3,2,1,0:T(8,128)S(1)}, u32[]{:S(2)}, u32[]{:S(2)}) collective-permute-start(f32[1,4,64,128]{3,2,1,0:T(8,128)S(1)} %get-tuple-element.137), channel_id=1, source_target_pairs={{0,1},{1,2},{2,3},{3,4},{4,5},{5,6},{6,7},{7,8},{8,9},{9,10},{10,1... | collective-permute-start | bytes 393224 | tf_op jit(solution)/shard_map/ppermute | solution.py:52
  126.0 32.8 %collective-permute-start.16 = (f32[6,8,1024]{2,1,0:T(8,128)}, f32[6,8,1024]{2,1,0:T(8,128)S(1)}, u32[]{:S(2)}, u32[]{:S(2)}) collective-permute-start(f32[6,8,1024]{2,1,0:T(8,128)} %get-tuple-element.129), channel_id=1, source_target_pairs={{0,6},{1,7},{2,4},{3,5},{4,2},{5,3},{6,0},{7,1},{8,14},{9,15},{10,... | collective-permute-start | bytes 589832 | tf_op jit(solution)/shard_map/ppermute | solution.py:52
  144.0 32.0 %collective-permute-start.29 = (f32[10,8,1024]{2,1,0:T(8,128)}, f32[10,8,1024]{2,1,0:T(8,128)S(1)}, u32[]{:S(2)}, u32[]{:S(2)}) collective-permute-start(f32[10,8,1024]{2,1,0:T(8,128)} %get-tuple-element.159), channel_id=1, source_target_pairs={{0,7},{1,6},{2,5},{3,4},{4,3},{5,2},{6,1},{7,0},{8,15},{9,14},{10,... | collective-permute-start | bytes 983048 | tf_op jit(solution)/shard_map/ppermute | solution.py:52
  148.3 28.7 %collective-permute-start.25 = (f32[10,8,1024]{2,1,0:T(8,128)}, f32[10,8,1024]{2,1,0:T(8,128)S(1)}, u32[]{:S(2)}, u32[]{:S(2)}) collective-permute-start(f32[10,8,1024]{2,1,0:T(8,128)} %get-tuple-element.151), channel_id=1, source_target_pairs={{0,6},{1,7},{2,4},{3,5},{4,2},{5,3},{6,0},{7,1},{8,14},{9,15},{10,... | collective-permute-start | bytes 983048 | tf_op jit(solution)/shard_map/ppermute | solution.py:52
  151.7 16.3 %collective-permute-start.21 = (f32[6,8,1024]{2,1,0:T(8,128)S(1)}, f32[6,8,1024]{2,1,0:T(8,128)S(1)}, u32[]{:S(2)}, u32[]{:S(2)}) collective-permute-start(f32[6,8,1024]{2,1,0:T(8,128)S(1)} %copy-done.31), channel_id=1, source_target_pairs={{0,3},{1,2},{2,1},{3,0},{4,7},{5,6},{6,5},{7,4},{8,11},{9,10},{10,... | collective-permute-start | bytes 589832 | tf_op jit(solution)/shard_map/ppermute | solution.py:52
  156.9 15.5 %collective-permute-start.19 = (f32[6,8,1024]{2,1,0:T(8,128)S(1)}, f32[6,8,1024]{2,1,0:T(8,128)S(1)}, u32[]{:S(2)}, u32[]{:S(2)}) collective-permute-start(f32[6,8,1024]{2,1,0:T(8,128)S(1)} %copy-done.30), channel_id=1, source_target_pairs={{0,2},{1,3},{2,0},{3,1},{4,6},{5,7},{6,4},{7,5},{8,10},{9,11},{10,... | collective-permute-start | bytes 589832 | tf_op jit(solution)/shard_map/ppermute | solution.py:52
  158.8 17.2 %collective-permute-start.17 = (f32[6,8,1024]{2,1,0:T(8,128)S(1)}, f32[6,8,1024]{2,1,0:T(8,128)S(1)}, u32[]{:S(2)}, u32[]{:S(2)}) collective-permute-start(f32[6,8,1024]{2,1,0:T(8,128)S(1)} %copy-done.29), channel_id=1, source_target_pairs={{0,1},{1,0},{2,3},{3,2},{4,5},{5,4},{6,7},{7,6},{8,9},{9,8},{10,11... | collective-permute-start | bytes 589832 | tf_op jit(solution)/shard_map/ppermute | solution.py:52
  172.4 18.3 %collective-permute-start.31 = (f32[10,8,1024]{2,1,0:T(8,128)}, f32[10,8,1024]{2,1,0:T(8,128)S(1)}, u32[]{:S(2)}, u32[]{:S(2)}) collective-permute-start(f32[10,8,1024]{2,1,0:T(8,128)} %get-tuple-element.162), channel_id=1, source_target_pairs={{0,5},{1,4},{2,7},{3,6},{4,1},{5,0},{6,3},{7,2},{8,13},{9,12},{10,... | collective-permute-start | bytes 983048 | tf_op jit(solution)/shard_map/ppermute | solution.py:52
  173.5 17.2 %collective-permute-start.28 = (f32[10,8,1024]{2,1,0:T(8,128)}, f32[10,8,1024]{2,1,0:T(8,128)S(1)}, u32[]{:S(2)}, u32[]{:S(2)}) collective-permute-start(f32[10,8,1024]{2,1,0:T(8,128)} %get-tuple-element.156), channel_id=1, source_target_pairs={{0,3},{1,2},{2,1},{3,0},{4,7},{5,6},{6,5},{7,4},{8,11},{9,10},{10,... | collective-permute-start | bytes 983048 | tf_op jit(solution)/shard_map/ppermute | solution.py:52
  176.0 29.1 %collective-permute-start.27 = (f32[10,8,1024]{2,1,0:T(8,128)}, f32[10,8,1024]{2,1,0:T(8,128)S(1)}, u32[]{:S(2)}, u32[]{:S(2)}) collective-permute-start(f32[10,8,1024]{2,1,0:T(8,128)} %get-tuple-element.154), channel_id=1, source_target_pairs={{0,2},{1,3},{2,0},{3,1},{4,6},{5,7},{6,4},{7,5},{8,10},{9,11},{10,... | collective-permute-start | bytes 983048 | tf_op jit(solution)/shard_map/ppermute | solution.py:52
  176.0 29.1 %collective-permute-start.30 = (f32[10,8,1024]{2,1,0:T(8,128)}, f32[10,8,1024]{2,1,0:T(8,128)S(1)}, u32[]{:S(2)}, u32[]{:S(2)}) collective-permute-start(f32[10,8,1024]{2,1,0:T(8,128)} %get-tuple-element.160), channel_id=1, source_target_pairs={{0,4},{1,5},{2,6},{3,7},{4,0},{5,1},{6,2},{7,3},{8,12},{9,13},{10,... | collective-permute-start | bytes 983048 | tf_op jit(solution)/shard_map/ppermute | solution.py:52
  177.0 28.1 %collective-permute-start.26 = (f32[10,8,1024]{2,1,0:T(8,128)}, f32[10,8,1024]{2,1,0:T(8,128)S(1)}, u32[]{:S(2)}, u32[]{:S(2)}) collective-permute-start(f32[10,8,1024]{2,1,0:T(8,128)} %get-tuple-element.152), channel_id=1, source_target_pairs={{0,1},{1,0},{2,3},{3,2},{4,5},{5,4},{6,7},{7,6},{8,9},{9,8},{10,11... | collective-permute-start | bytes 983048 | tf_op jit(solution)/shard_map/ppermute | solution.py:52
  (32 other events, 487.8 us)
